TPU v7x, 32 devices: a whole 2x2x4 slice. The times are simulated.
32 devices in a mesh: gx: 2 (over y), gy: 4 (over x, core), gz: 4 (over z).
Axes of the slice: x: 2, y: 2, z: 4, core: 2. Of those that a mesh axis runs over, the one named last changes fastest.
Arguments:
- volume: bfloat16 [32, 16, 32, 128], P('gz', 'gx', 'gy'), may hold values from -6 to 6
- cotangent: bfloat16 [32, 16, 32, 128], P('gz', 'gx', 'gy'), may hold values from -0.125 to 0.125
- w_conv: bfloat16 [128, 27, 128], replicated, may hold values from -0.109375 to 0.109375
- w_down: bfloat16 [8, 128, 512], replicated, may hold values from -0.25 to 0.25
- w_bottle: bfloat16 [512, 27, 512], P(None, None, 'gz'), may hold values from -0.0546875 to 0.0546875
- w_up: bfloat16 [8, 512, 128], replicated, may hold values from -0.375 to 0.375
Outputs:
- output: bfloat16 [32, 16, 32, 128], P('gz', 'gx', 'gy')
- grad_conv: float32 [128, 27, 128], P(('gx', 'gy'))
- grad_bottle: float32 [512, 27, 512], P(('gx', 'gy'), None, 'gz')
All inputs are finite; a program needn't handle non-finite values.
Results may differ from a plain program's by a relative error of at most 0.015.
Values may be sent and summed in bfloat16 or wider, within the bound.
No kernel may reach another device: no remote copies, remote signals or barrier semaphores. Data moves between devices by JAX's collectives and lax.ppermute only.
A program may use at most 64 MiB of HBM per device.

v0:
```python
import numpy as np
import jax
import jax.numpy as jnp
from jax import lax
from jax.experimental import pallas as pl
from jax.experimental.pallas import tpu as pltpu
from jax.sharding import PartitionSpec as P

BF16 = jnp.bfloat16
F32 = jnp.float32
VMEM_LIMIT = 24 * 1024 * 1024


def local_call(kernel, name, out_shapes, scratch=(), flops=300_000_000):
    whole = pl.BlockSpec(memory_space=pltpu.VMEM)

    def call(*operands):
        return pl.pallas_call(
            kernel,
            name=name,
            out_shape=out_shapes,
            in_specs=[whole] * len(operands),
            out_specs=jax.tree.map(lambda _: whole, out_shapes),
            scratch_shapes=list(scratch),
            compiler_params=pltpu.CompilerParams(vmem_limit_bytes=VMEM_LIMIT),
            cost_estimate=pl.CostEstimate(flops=flops, bytes_accessed=flops // 1000, transcendentals=0),
        )(*operands)

    return call


def matmul(left, right):
    return jnp.dot(left, right, preferred_element_type=F32)


def matmul_nt(left, right):
    return lax.dot_general(left, right, (((1,), (1,)), ((), ())), preferred_element_type=F32)


def sub_order(size_x, size_y):
    half_x, half_y = size_x // 2, size_y // 2
    return {
        (2 * kx + b, 2 * ky + c): ((2 * b + c) * half_x + kx) * half_y + ky
        for b in range(2)
        for c in range(2)
        for kx in range(half_x)
        for ky in range(half_y)
    }


def fine_maps(size_x, size_y):
    own = size_x * size_y
    rows = sub_order(size_x, size_y)
    order = np.zeros((own, own), np.float32)
    taps = np.zeros((9, own, 2 * own), np.float32)
    for (x, y), row in rows.items():
        order[row, x * size_y + y] = 1
        for b in range(3):
            for c in range(3):
                sx, sy = x + b - 1, y + c - 1
                if sx < 0:
                    part = 0 if 0 <= sy < size_y else (4 if sy < 0 else 5)
                    source = own + 8 * part + sy % size_y
                elif sx >= size_x:
                    part = 1 if 0 <= sy < size_y else (6 if sy < 0 else 7)
                    source = own + 8 * part + sy % size_y
                elif sy < 0:
                    source = own + 16 + sx
                elif sy >= size_y:
                    source = own + 24 + sx
                else:
                    source = sx * size_y + sy
                taps[3 * b + c, row, source] = 1
    return order, taps


def coarse_maps(count_x, count_y, half_x, half_y):
    wide_x, wide_y = count_x * half_x, count_y * half_y

    def row_of(x, y):
        brick = (x // half_x) * count_y + y // half_y
        return (brick * half_x + x % half_x) * half_y + y % half_y

    shift = np.zeros((9, wide_x * wide_y, wide_x * wide_y), np.float32)
    for x in range(wide_x):
        for y in range(wide_y):
            for b in range(3):
                for c in range(3):
                    sx, sy = x + b - 1, y + c - 1
                    if 0 <= sx < wide_x and 0 <= sy < wide_y:
                        shift[3 * b + c, row_of(x, y), row_of(sx, sy)] = 1
    return shift


def column_maps(half_x, half_y, depth):
    quarter = half_x * half_y
    rows = depth * quarter
    send = np.zeros((2, depth * (half_y + 2 * half_x + 2), rows), np.float32)
    rim = np.zeros((2, 9, 4, quarter, 8 * quarter), np.float32)
    for px in range(2):
        edge = 0 if px else half_x - 1
        for z in range(depth):
            base = z * quarter
            for ky in range(half_y):
                send[px, z * half_y + ky, base + edge * half_y + ky] = 1
            for side, ky in enumerate((0, half_y - 1)):
                row = depth * (half_y + side * half_x) + z * half_x
                for kx in range(half_x):
                    send[px, row + kx, base + kx * half_y + ky] = 1
                send[px, depth * (half_y + 2 * half_x + side) + z, base + edge * half_y + ky] = 1
    for px in range(2):
        for b in range(3):
            for c in range(3):
                for kx in range(half_x):
                    for ky in range(half_y):
                        sx, sy = kx + b - 1, ky + c - 1
                        beyond = sx < 0 if px else sx >= half_x
                        if (sx < 0 or sx >= half_x) and not beyond:
                            continue
                        for z in range(4):
                            if beyond and 0 <= sy < half_y:
                                source = 4 * quarter + z * half_y + sy
                            elif beyond:
                                source = 7 * quarter + 4 * (sy >= half_y) + z
                            elif sy < 0:
                                source = 5 * quarter + z * half_x + sx
                            elif sy >= half_y:
                                source = 6 * quarter + z * half_x + sx
                            else:
                                source = z * quarter + sx * half_y + sy
                            rim[px, 3 * b + c, z, kx * half_y + ky, source] = 1
    return send, rim


def swap(block, axes, count, distance):
    return lax.ppermute(block, axes, [(i, i ^ distance) for i in range(count)])


def trade(blocks, axes, count):
    got = {d: swap(blocks[d], axes, count, d) for d in reversed(range(1, count))}
    return [blocks[0]] + [got[d] for d in range(1, count)]


def line_pairs(length):
    first = [(i, i ^ 1) for i in range(length)]
    second = [(i, i + 1 if i % 2 else i - 1) for i in range(1, length - 1)]
    return first, second


def swap_rims(x_send, send_b, corner_b, counts):
    count_x, count_y, _ = counts
    axes, count = ("gx", "gy"), count_x * count_y
    corner = swap(corner_b, axes, count, count_y + 2)
    x_rim = swap(x_send, axes, count, count_y)
    across = swap(send_b, axes, count, 2)
    return x_rim, across, corner


def line_sides(axis, pair_a, pair_b):
    even = lax.axis_index(axis) % 2 == 0
    return jnp.where(even, pair_b, pair_a), jnp.where(even, pair_a, pair_b)


def relay_rims_kernel(corner, across, x_rim, send_a, send, side):
    face, lines = across.shape[0], corner.shape[0]
    pitch = x_rim.shape[0] // lines
    even = lax.axis_index("gy") % 2 == 0
    for part in range(0, x_rim.shape[1], 128):
        columns = slice(part, part + 128)
        side[...] = x_rim[:, columns].astype(F32)
        ends = [side[pl.ds(y, lines, stride=pitch), :] for y in (pitch - 1, 0)]
        send[face + lines : face + 2 * lines, columns] = jnp.where(even, ends[0], ends[1]).astype(BF16)
    send[face + 2 * lines :, :] = send_a[...]
    send[:face, :] = across[...]
    send[face : face + lines, :] = corner[...]


def pass_kernel(block, out):
    out[...] = block[...]


def relay_rims(x_rim, across, corner, send_a, counts):
    rows = 2 * (across.shape[0] + corner.shape[0])
    corner = local_call(pass_kernel, "corner", shape_of(corner.shape), flops=5_000_000_000)(corner)
    send = local_call(
        relay_rims_kernel,
        "relay_rims",
        shape_of((rows, across.shape[1])),
        [pltpu.VMEM((x_rim.shape[0], 128), F32)],
    )(corner, across, x_rim, send_a)
    return swap(send, ("gx", "gy"), counts[0] * counts[1], 1)


def y_rims(relayed, lines):
    py = lax.axis_index("gy")
    face = relayed.shape[0] // 2 - lines
    inner = (py > 0) & (py < lax.axis_size("gy") - 1)
    face_b = jnp.where(inner, relayed[:face, :].astype(F32), 0.0)
    corner_b = jnp.where(inner, relayed[face : face + lines, :].astype(F32), 0.0)
    corner_a = relayed[face + lines : face + 2 * lines, :].astype(F32)
    face_a = relayed[face + 2 * lines :, :].astype(F32)
    return *line_sides("gy", face_a, face_b), *line_sides("gy", corner_a, corner_b)


def plane_index(count_y):
    return lax.axis_index("gx") * count_y + lax.axis_index("gy")


def plane_rows(ref, z):
    _, size_x, size_y, channels = ref.shape
    return ref[z].astype(F32).reshape(size_x * size_y, channels)


def hand_out(blocks, outs, me):
    for d, out in enumerate(outs):
        out[...] = blocks[me ^ d]


def take_in(parts, blocks, me):
    for d, part in enumerate(parts):
        blocks[me ^ d] = part[...]


def total_of(parts):
    terms = [part[...].astype(F32) for part in parts]
    while len(terms) > 1:
        terms = [terms[i] + terms[i + 1] for i in range(0, len(terms), 2)]
    return terms[0]


def back_kernel(count_z, cotangent, w_up, order, *refs):
    sends, (ordered, blocks) = refs[:count_z], refs[count_z:]
    size_z, size_x, size_y, channels = cotangent.shape
    own = size_x * size_y
    quarter = own // 4
    for z in range(size_z):
        ordered[z] = matmul(order[...], plane_rows(cotangent, z).astype(BF16)).astype(BF16)
    back = None
    for s in range(8):
        a, bc = s // 4, s % 4
        cells = jnp.concatenate(
            [ordered[2 * kz + a, bc * quarter : (bc + 1) * quarter, :] for kz in range(size_z // 2)], axis=0
        )
        term = matmul_nt(cells, w_up[s])
        back = term if back is None else back + term
    back = back.astype(BF16)
    group = back.shape[1] // count_z
    for q in range(count_z):
        blocks[q] = back[:, q * group : (q + 1) * group]
    hand_out(blocks, sends, lax.axis_index("gz"))


def deepen(volume, z_a, z_b, deep, pitch):
    size_z, size_x, size_y, channels = volume.shape
    own = size_x * size_y
    below, above = line_sides("gz", z_a[...], z_b[...])
    deep[:own, :] = below.astype(F32).reshape(own, channels)
    for z in range(size_z):
        deep[(z + 1) * pitch : (z + 1) * pitch + own, :] = plane_rows(volume, z)
    deep[(size_z + 1) * pitch : (size_z + 1) * pitch + own, :] = above.astype(F32).reshape(own, channels)


def ends_kernel(volume, send_a, send_b):
    below, above = volume[0], volume[volume.shape[0] - 1]
    send_b[...], send_a[...] = line_sides("gz", above, below)


def faces_kernel(volume, z_a, z_b, x_send, send_a, send_b, corner_b, deep):
    size_z, size_x, size_y, channels = volume.shape
    own = size_x * size_y
    planes = x_send.shape[0] // size_y
    deepen(volume, z_a, z_b, deep, own)
    start = (size_z + 2) * own
    deep[start:, :] = jnp.zeros((deep.shape[0] - start, channels), F32)
    first = lax.axis_index("gx") == 0
    far = (size_x - 1) * size_y

    def x_face(start):
        return jnp.concatenate([deep[z * own + start : z * own + start + size_y, :] for z in range(planes)], axis=0)

    x_send[...] = jnp.where(first, x_face(far), x_face(0)).astype(BF16)
    faces, corners = [], []
    for y in (0, size_y - 1):
        faces.append(deep[pl.ds(y, send_a.shape[0], stride=size_y), :].astype(BF16))
        ends = [deep[pl.ds(start + y, planes, stride=own), :] for start in (far, 0)]
        corners.append(jnp.where(first, ends[0], ends[1]).astype(BF16))
    send_b[...], send_a[...] = line_sides("gy", faces[1], faces[0])
    corner_b[...], _ = line_sides("gy", corners[1], corners[0])


def hidden_kernel(count_z, volume, z_a, z_b, x_rim, relayed, taps, w_conv, w_down, *refs):
    backs, (hidden, slope, rim), sends, (rim32, cells) = (
        refs[:count_z],
        refs[count_z : count_z + 3],
        refs[count_z + 3 : -2],
        refs[-2:],
    )
    size_z, size_x, size_y, channels = volume.shape
    own = size_x * size_y
    quarter = own // 4
    planes = size_z + 2
    pitch = 2 * own
    first = lax.axis_index("gx") == 0
    deepen(volume, z_a, z_b, rim32, pitch)
    y_low, y_high, xy_low, xy_high = y_rims(relayed, x_rim.shape[0] // size_y)
    x_side = x_rim[...].astype(F32)
    x_low, x_high = jnp.where(first, 0.0, x_side), jnp.where(first, x_side, 0.0)
    faces = (x_low, x_high, y_low, y_high)
    for z in range(planes):
        for part, block in enumerate(faces):
            start = z * pitch + own + 8 * part
            rim32[start : start + 8, :] = block[8 * z : 8 * (z + 1), :]
        rim32[z * pitch + own + 32 : (z + 1) * pitch, :] = jnp.zeros((own - 32, channels), F32)
    corners = ((xy_low, 7, True), (xy_high, 0, True), (xy_low, 7, False), (xy_high, 0, False))
    for part, (block, row, low) in enumerate(corners):
        start = own + 32 + 8 * part + row
        value = jnp.where(first == low, 0.0, block)
        rim32[pl.ds(start, 8, stride=pitch), :] = value[:8, :]
        for z in range(8, planes):
            rim32[z * pitch + start : z * pitch + start + 1, :] = value[z : z + 1, :]
    for z in range(0, planes, 2):
        pair = [rim32[(z + i) * pitch : (z + i + 1) * pitch, :].astype(BF16) for i in range(2)]
        moved = matmul(taps[...], jnp.concatenate(pair, axis=1)).astype(BF16)
        for i in range(2):
            rim[z + i] = pair[i]
            for bc in range(9):
                cells[z + i, :, bc * channels : (bc + 1) * channels] = moved[
                    bc * own : (bc + 1) * own, i * channels : (i + 1) * channels
                ]
    weights = [w_conv[9 * a : 9 * (a + 1)].reshape(9 * channels, channels) for a in range(3)]
    window = cells[: size_z + 1].reshape((size_z + 1) * own, 9 * channels)
    both = matmul(window, jnp.concatenate(weights[:2], axis=1))
    window = cells[2:].reshape(size_z * own, 9 * channels)
    pre = both[:-own, :channels] + both[own:, channels:] + matmul(window, weights[2])
    sig = jax.nn.sigmoid(pre)
    slope[...] = (sig * (1.0 + pre * (1.0 - sig))).reshape(size_z, own, channels)
    hidden[...] = (pre * sig).astype(BF16).reshape(size_z, own, channels)
    parts = []
    for s in range(8):
        a, bc = s // 4, s % 4
        parts.append(
            jnp.concatenate(
                [hidden[2 * kz + a, bc * quarter : (bc + 1) * quarter, :] for kz in range(size_z // 2)], axis=0
            )
        )
    coarse = matmul(jnp.concatenate(parts, axis=1), w_down[...].reshape(8 * channels, w_down.shape[2]))
    coarse = coarse.astype(BF16)
    wide = coarse.shape[1]
    for send, back in zip(sends, backs):
        send[:, :wide] = coarse
        send[:, wide:] = back[...]


def rim_transpose_kernel(count_p, rim, taps_t, turned):
    planes, rows, channels = rim.shape
    share = channels // count_p
    for pair in range(planes // 2):
        sides = [rim[2 * pair + i].astype(F32).T for i in range(2)]
        moved = matmul(jnp.concatenate(sides, axis=1).astype(BF16), taps_t[...]).astype(BF16)
        for bc in range(9):
            for p in range(count_p):
                start = (bc * count_p // 2 + p // 2) * share
                turned[p % 2, start : start + share, pair * rows : (pair + 1) * rows] = moved[
                    p * share : (p + 1) * share, bc * rows : (bc + 1) * rows
                ]


def column_kernel(count_z, *refs):
    parts, picks, (column, back, x_send, send_a, send_b, corner_b) = refs[:count_z], refs[count_z], refs[count_z + 1 :]
    own_cells = parts[0].shape[0]
    wide = column.shape[1]
    pz = lax.axis_index("gz")
    for i, part in enumerate(parts):
        rows = pl.ds(pl.multiple_of((pz ^ (-i % count_z)) * own_cells, own_cells), own_cells)
        column[rows, :] = part[:, :wide]
        back[rows, :] = part[:, wide:]
    rims = matmul(picks[lax.axis_index("gx")], column[...]).astype(BF16)
    cuts, start = [], 0
    for size in (x_send.shape[0], *[send_a.shape[0]] * 2, *[corner_b.shape[0]] * 2):
        cuts.append(rims[start : start + size, :])
        start += size
    x_send[...] = cuts[0]
    send_b[...], send_a[...] = line_sides("gy", cuts[2], cuts[1])
    corner_b[...], _ = line_sides("gy", cuts[4], cuts[3])


def bottle_kernel(quarter, column, back, x_rim, relayed, shift, w_bottle, *refs):
    count = len(refs) // 2 - 1
    slices, bottle, sends, (corners, window) = refs[:count], refs[count], refs[count + 1 : -2], refs[-2:]
    cells, wide = column.shape
    outs = w_bottle.shape[2]
    side = x_rim.shape[0]
    depth = cells // quarter
    span = 4 * quarter
    picks = shift[lax.axis_index("gx")]
    window[:quarter, :] = jnp.zeros((quarter, 9 * wide), BF16)
    window[(depth + 1) * quarter :, :] = jnp.zeros((quarter, 9 * wide), BF16)
    edge = side // (depth // 4)
    y_low, y_high, xy_low, xy_high = y_rims(relayed, depth)
    y_low, y_high = y_low.astype(BF16), y_high.astype(BF16)
    for g in range(depth // 4):
        corners[g, :4, :] = xy_low[4 * g : 4 * g + 4, :]
        corners[g, 4:8, :] = xy_high[4 * g : 4 * g + 4, :]
        corners[g, 8:, :] = jnp.zeros((8, wide), F32)
        faces = [block[g * edge : (g + 1) * edge, :] for block in (x_rim, y_low, y_high)]
        rows = [column[g * span : (g + 1) * span, :], *faces, corners[g].astype(BF16)]
        moved = matmul(picks, jnp.concatenate(rows, axis=0)).astype(BF16)
        for bc in range(9):
            window[quarter + g * span : quarter + (g + 1) * span, bc * wide : (bc + 1) * wide] = moved[
                bc * span : (bc + 1) * span, :
            ]
    both = pre = None
    for bc in range(9):
        part = slice(bc * wide, (bc + 1) * wide)
        weight = jnp.concatenate([w_bottle[bc], w_bottle[9 + bc]], axis=1)
        term = matmul(window[: cells + quarter, part], weight)
        both = term if both is None else both + term
        term = matmul(window[2 * quarter :, part], w_bottle[18 + bc])
        pre = term if pre is None else pre + term
    pre = pre + both[:cells, :outs] + both[quarter:, outs:]
    sig = jax.nn.sigmoid(pre)
    bottle[...] = (pre * sig).astype(BF16)
    slope = sig * (1.0 + pre * (1.0 - sig))
    value = (back[...].astype(F32) * slope).astype(BF16)
    for send, block in zip(sends, slices):
        send[:cells, :] = value
        send[cells:, :] = block[...]


def slices_kernel(count_y, quarter, column, *refs):
    sends, slices = refs[:-1], refs[-1]
    cells, wide = column.shape
    span = 4 * quarter
    half = 2 * quarter
    lane = lax.broadcasted_iota(jnp.int32, (half, 128), 1)
    for pair in range(wide // 128):
        for g in range(cells // span):
            top = column[g * span : g * span + half, pair * 128 : (pair + 1) * 128].astype(F32)
            end = column[g * span + half : (g + 1) * span, pair * 128 : (pair + 1) * 128].astype(F32)
            rows = slice(g * half, (g + 1) * half)
            slices[2 * pair, rows, :] = jnp.where(lane < 64, top, pltpu.roll(end, 64, 1)).astype(BF16)
            slices[2 * pair + 1, rows, :] = jnp.where(lane < 64, pltpu.roll(top, 64, 1), end).astype(BF16)
    p = plane_index(count_y)
    lines = slices.shape[1]
    for i, send in enumerate(sends):
        send[:lines, :] = slices[p ^ (2 * i)]
        send[lines:, :] = slices[p ^ (2 * i + 1)]


def coarse_grad_kernel(count_y, count_z, quarter, *refs):
    grads, (bottle, shift, w_bottle) = refs[: -count_z - 6], refs[-count_z - 6 : -count_z - 3]
    sends, (window, gathered, blocks) = refs[-count_z - 3 : -3], refs[-3:]
    count_p = len(grads)
    cells, outs = bottle.shape
    rows = count_p * quarter
    depth = cells // quarter
    own_cells = cells // count_z
    inputs = w_bottle.shape[1]
    p = plane_index(count_y)
    for i, part in enumerate(grads):
        gathered[p ^ (-i % count_p)] = part[:cells, :]
    mine = pl.multiple_of(p * quarter, quarter)
    picks = jnp.concatenate([shift[pl.ds((8 - bc) * rows + mine, quarter), :] for bc in range(9)], axis=0)
    window[:quarter, :] = jnp.zeros((quarter, 9 * outs), BF16)
    window[(depth + 1) * quarter :, :] = jnp.zeros((quarter, 9 * outs), BF16)
    for z in range(depth):
        plane = jnp.concatenate([gathered[q, z * quarter : (z + 1) * quarter, :] for q in range(count_p)], axis=0)
        moved = matmul(picks, plane).astype(BF16)
        for bc in range(9):
            window[(z + 1) * quarter : (z + 2) * quarter, bc * outs : (bc + 1) * outs] = moved[
                bc * quarter : (bc + 1) * quarter, :
            ]
    total = None
    for a in range(3):
        weight = jnp.concatenate([w_bottle[9 * a + bc] for bc in range(9)], axis=1)
        term = matmul_nt(window[(2 - a) * quarter : (2 - a + depth) * quarter, :], weight)
        total = term if total is None else total + term
    total = total.astype(BF16)
    for q in range(count_z):
        blocks[q, :, :inputs] = total[q * own_cells : (q + 1) * own_cells, :]
        blocks[q, :, inputs:] = bottle[q * own_cells : (q + 1) * own_cells, :]
    hand_out(blocks, sends, lax.axis_index("gz"))


def wide_kernel(count_y, quarter, *refs):
    parts, (wide, grads) = refs[:-2], refs[-2:]
    count_p, cells, outs = grads.shape
    rows = count_p * quarter
    depth = cells // quarter
    take_in([part.at[:cells, :] for part in parts], grads, plane_index(count_y))
    planes = [
        jnp.concatenate([grads[q, z * quarter : (z + 1) * quarter, :] for q in range(count_p)], axis=0)
        for z in range(depth)
    ]
    zeros = jnp.zeros((rows, outs), BF16)
    for j in range(depth // 2):
        for slot in range(5):
            z = j // 2 * 4 + j % 2 + slot - 1
            wide[j * rows : (j + 1) * rows, slot * outs : (slot + 1) * outs] = planes[z] if 0 <= z < depth else zeros


def coarse_transpose_kernel(count_y, shift, *refs):
    parts, (turned, slices) = refs[:-2], refs[-2:]
    count_p, lines, _ = slices.shape
    rows = shift.shape[1]
    quarter = rows // count_p
    p = plane_index(count_y)
    for d, part in enumerate(parts):
        start = (2 + d % 2) * lines
        slices[p ^ d] = part[start : start + lines, :]
    for j in range(lines // quarter):
        plane = jnp.concatenate([slices[q, j * quarter : (j + 1) * quarter, :] for q in range(count_p)], axis=0)
        plane = plane.astype(F32).T.astype(BF16)
        for bc in range(9):
            turned[bc * 128 : (bc + 1) * 128, j * rows : (j + 1) * rows] = matmul(
                plane, shift[(8 - bc) * rows : (9 - bc) * rows, :]
            ).astype(BF16)


def grad_bottle_kernel(turned, wide, out):
    _, channels, outs = out.shape
    full = matmul(turned[...], wide[...])
    for bc in range(9):
        top = full[bc * 128 : bc * 128 + channels, :]
        end = full[bc * 128 + channels : (bc + 1) * 128, :]
        for a in range(3):
            out[9 * a + bc] = top[:, (2 - a) * outs : (3 - a) * outs] + end[:, (4 - a) * outs : (5 - a) * outs]


def half_grad(turned, shifted, parity, chip, out, blocks):
    chips, rows, channels = blocks.shape
    group = rows // 27
    full = matmul(turned[parity], shifted[...])
    for bc in range(9):
        for a in range(3):
            t = 9 * a + bc
            for q in range(chips):
                start = (bc * chips + q) * group
                blocks[q, t * group : (t + 1) * group, :] = full[
                    start : start + group, a * channels : (a + 1) * channels
                ].astype(BF16)
    for i in range(chips):
        out[i] = blocks[chip ^ i]


def hidden_grad_kernel(count_y, count_z, *refs):
    parts, (slope, ordered, w_down, turned) = refs[:count_z], refs[count_z : count_z + 4]
    shifted, bottle, give, bottles, blocks = refs[count_z + 4 :]
    size_z, own, channels = ordered.shape
    quarter = own // 4
    inputs = w_down.shape[2]
    pz = lax.axis_index("gz")
    grad = total_of([part.at[:, :inputs] for part in parts]).astype(BF16)
    for i, part in enumerate(parts):
        bottles[pz ^ (-i % count_z)] = part[:, inputs:]
    bottle[...] = jnp.concatenate([bottles[q] for q in range(count_z)], axis=1)
    shifted[...] = jnp.zeros_like(shifted)
    for s in range(8):
        a, bc = s // 4, s % 4
        spread_grad = matmul_nt(grad, w_down[s])
        for kz in range(size_z // 2):
            z = 2 * kz + a
            part = slice(bc * quarter, (bc + 1) * quarter)
            line = slice(kz * quarter, (kz + 1) * quarter)
            value = ((spread_grad[line, :] + ordered[z, part, :].astype(F32)) * slope[z, part, :]).astype(BF16)
            for t in range(3):
                start = (z + t) * own + bc * quarter
                shifted[start : start + quarter, t * channels : (t + 1) * channels] = value
    p = plane_index(count_y)
    half_grad(turned, shifted, 1 - p % 2, p // 2, give, blocks)


def keep_kernel(count_y, shifted, turned, keep, blocks):
    p = plane_index(count_y)
    half_grad(turned, shifted, p % 2, p // 2, keep, blocks)


def output_kernel(bottle, hidden, w_up, order_t, output, rows_out):
    size_z, own, channels = hidden.shape
    quarter = own // 4
    for s in range(8):
        a, bc = s // 4, s % 4
        lifted = matmul(bottle[...], w_up[s])
        for kz in range(size_z // 2):
            z = 2 * kz + a
            part = slice(bc * quarter, (bc + 1) * quarter)
            line = slice(kz * quarter, (kz + 1) * quarter)
            rows_out[z, part, :] = (lifted[line, :] + hidden[z, part, :].astype(F32)).astype(BF16)
    for z in range(size_z):
        plane = matmul(order_t[...], rows_out[z])
        output[z] = plane.reshape(output.shape[1:]).astype(BF16)


def pair_sum_kernel(keep, got, *sends):
    for i, send in enumerate(sends):
        send[...] = (keep[i].astype(F32) + got[i].astype(F32)).astype(BF16)


def sum_kernel(*refs):
    out = refs[-1]
    out[...] = total_of(refs[:-1]).reshape(out.shape).astype(out.dtype)


def shape_of(shape, dtype=BF16):
    return jax.ShapeDtypeStruct(shape, dtype)


def gathered_body(counts, volume, cotangent, w_conv, w_down, w_bottle, w_up):
    count_x, count_y, count_z = counts
    count_p = count_x * count_y
    size_z, size_x, size_y, channels = volume.shape
    wide = w_down.shape[2]
    group = w_bottle.shape[2]
    half_x, half_y = size_x // 2, size_y // 2
    own = size_x * size_y
    quarter = half_x * half_y
    own_cells = size_z // 2 * quarter
    cells = count_z * own_cells
    depth = count_z * size_z // 2
    rows = count_p * quarter
    planes = size_z + 2
    share_c = channels // count_p
    share_w = wide // count_p
    plane_axes = ("gx", "gy")

    order, taps = fine_maps(size_x, size_y)
    pair_taps = np.zeros((2, 2 * own, 9, 2, own), np.float32)
    for i in range(2):
        pair_taps[i, :, :, i, :] = taps.transpose(2, 0, 1)
    shift = coarse_maps(count_x, count_y, half_x, half_y)
    order_m = jnp.asarray(order, BF16)
    order_t = jnp.asarray(order.T, BF16)
    taps_m = jnp.asarray(taps.reshape(9 * own, 2 * own), BF16)
    taps_t = jnp.asarray(pair_taps.reshape(4 * own, 18 * own), BF16)
    shift_m = jnp.asarray(shift.reshape(9 * rows, rows), BF16)

    send_maps, rim_maps = column_maps(half_x, half_y, depth)
    send_m = jnp.asarray(send_maps, BF16)
    rim_m = jnp.asarray(rim_maps.reshape(count_x, 36 * quarter, 8 * quarter), BF16)

    w_conv_t = jnp.transpose(w_conv, (1, 0, 2))
    w_bottle_t = jnp.transpose(w_bottle, (1, 0, 2))
    send_a, send_b = local_call(ends_kernel, "ends", [shape_of((size_x, size_y, channels))] * 2)(volume)
    z_pairs = line_pairs(count_z)
    z_b = lax.ppermute(send_b, "gz", z_pairs[1])
    z_a = lax.ppermute(send_a, "gz", z_pairs[0])
    *backs, ordered = local_call(
        lambda *refs: back_kernel(count_z, *refs),
        "back",
        [shape_of((own_cells, group))] * count_z + [shape_of((size_z, own, channels))],
        [pltpu.VMEM((count_z, own_cells, group), BF16)],
    )(cotangent, w_up, order_m)
    sends = local_call(
        faces_kernel,
        "faces",
        [shape_of((16 * size_y, channels))] + [shape_of((planes * size_x, channels))] * 2 + [shape_of((16, channels))],
        [pltpu.VMEM((16 * own, channels), F32)],
    )(volume, z_a, z_b)
    x_send, send_a, send_b, corner_b = sends
    x_rim, across, corner = swap_rims(x_send, send_b, corner_b, counts)
    relayed = relay_rims(x_rim, across, corner, send_a, counts)
    hidden, slope, rim, *sends = local_call(
        lambda *refs: hidden_kernel(count_z, *refs),
        "hidden",
        [
            shape_of((size_z, own, channels)),
            shape_of((size_z, own, channels), F32),
            shape_of((planes, 2 * own, channels)),
        ]
        + [shape_of((own_cells, wide + group))] * count_z,
        [
            pltpu.VMEM((planes * 2 * own, channels), F32),
            pltpu.VMEM((planes, own, 9 * channels), BF16),
        ],
        flops=2_000_000_000,
    )(volume, z_a, z_b, x_rim, relayed, taps_m, w_conv_t, w_down, *backs)
    parts = trade(sends, "gz", count_z)
    column, back, *sends = local_call(
        lambda *refs: column_kernel(count_z, *refs),
        "column",
        [shape_of((cells, wide)), shape_of((cells, group)), shape_of((depth * half_y, wide))]
        + [shape_of((depth * half_x, wide))] * 2
        + [shape_of((depth, wide))],
    )(parts[0], *parts[:0:-1], send_m)
    x_send, send_a, send_b, corner_b = sends
    x_rim, across, corner = swap_rims(x_send, send_b, corner_b, counts)
    relayed = relay_rims(x_rim, across, corner, send_a, counts)
    slices = local_call(
        lambda *refs: slices_kernel(count_y, quarter, *refs),
        "slices",
        [shape_of((cells, 128))] * (count_p // 2),
        [pltpu.VMEM((count_p, cells // 2, 128), BF16)],
    )(column)
    column, *slices = lax.optimization_barrier((column, *slices))
    bottle, *sends = local_call(
        lambda *refs: bottle_kernel(quarter, *refs),
        "bottle",
        [shape_of((cells, group))] + [shape_of((2 * cells, group))] * (count_p // 2),
        [
            pltpu.VMEM((depth // 4, 16, wide), F32),
            pltpu.VMEM(((depth + 2) * quarter, 9 * wide), BF16),
        ],
        flops=2_000_000_000,
    )(column, back, x_rim, relayed, rim_m, w_bottle_t, *slices)
    grads = [None] * count_p
    grads[0] = sends[0]
    for d in (6, 4, 2):
        grads[d] = swap(sends[d // 2], plane_axes, count_p, d)
    for d in (0, 2, 4, 6):
        grads[d + 1] = swap(grads[d], plane_axes, count_p, 1)
    sends = local_call(
        lambda *refs: coarse_grad_kernel(count_y, count_z, quarter, *refs),
        "coarse_grad",
        [shape_of((own_cells, wide + group))] * count_z,
        [
            pltpu.VMEM(((depth + 2) * quarter, 9 * group), BF16),
            pltpu.VMEM((count_p, cells, group), BF16),
            pltpu.VMEM((count_z, own_cells, wide + group), BF16),
        ],
    )(grads[0], *grads[:0:-1], bottle, shift_m, w_bottle_t)
    parts = trade(sends, "gz", count_z)
    rim, late, _ = lax.optimization_barrier((rim, grads[0], sends[1]))
    turned = local_call(
        lambda *refs: rim_transpose_kernel(count_p, *refs),
        "rim_transpose",
        shape_of((2, 9 * channels // 2, planes * own)),
    )(rim, taps_t)
    coarse_turned = local_call(
        lambda *refs: coarse_transpose_kernel(count_y, *refs),
        "coarse_transpose",
        shape_of((18 * share_w, depth // 2 * rows)),
        [pltpu.VMEM((count_p, cells // 2, 128), BF16)],
    )(shift_m, late, *grads[1:])
    turned, coarse_turned = lax.optimization_barrier((turned, coarse_turned))
    shifted, bottle, give = local_call(
        lambda *refs: hidden_grad_kernel(count_y, count_z, *refs),
        "hidden_grad",
        [
            shape_of((planes * own, 3 * channels)),
            shape_of((own_cells, wide)),
            shape_of((count_p // 2, 27 * share_c, channels)),
        ],
        [
            pltpu.VMEM((count_z, own_cells, group), BF16),
            pltpu.VMEM((count_p // 2, 27 * share_c, channels), BF16),
        ],
    )(parts[0], *parts[:0:-1], slope, ordered, w_down, turned)
    got = swap(give, plane_axes, count_p, 1)
    keep = local_call(
        lambda *refs: keep_kernel(count_y, *refs),
        "keep",
        shape_of((count_p // 2, 27 * share_c, channels)),
        [pltpu.VMEM((count_p // 2, 27 * share_c, channels), BF16)],
    )(shifted, turned)
    output = local_call(
        output_kernel,
        "output",
        shape_of(volume.shape),
        [pltpu.VMEM((size_z, own, channels), BF16)],
    )(bottle, hidden, w_up, order_t)
    sends = local_call(
        pair_sum_kernel,
        "pair_sum",
        [shape_of((27 * share_c, channels))] * (count_p // 2),
    )(keep, got)
    parts = [sends[0]] + [swap(sends[d // 2], plane_axes, count_p, d) for d in (6, 4, 2)]
    part = local_call(sum_kernel, "plane_sum", shape_of((27 * share_c, channels)))(*parts)
    part, output = lax.optimization_barrier((part, output))
    got = swap(part, "gz", count_z, 1)
    wide_grads = local_call(
        lambda *refs: wide_kernel(count_y, quarter, *refs),
        "wide",
        shape_of((depth // 2 * rows, 5 * group)),
        [pltpu.VMEM((count_p, cells, group), BF16)],
    )(*grads)
    got, wide_grads = lax.optimization_barrier((got, wide_grads))
    part = local_call(sum_kernel, "depth_sum", shape_of((27 * share_c, channels)))(part, got)
    got = swap(part, "gz", count_z, 2)
    grad_bottle = local_call(
        grad_bottle_kernel,
        "grad_bottle",
        shape_of((27, share_w, group), F32),
        flops=4_000_000_000,
    )(coarse_turned, wide_grads)
    grad_conv = local_call(
        sum_kernel,
        "grad_conv",
        shape_of((27, share_c, channels), F32),
    )(part, got)
    return (output, jnp.transpose(grad_conv, (1, 0, 2)), jnp.transpose(grad_bottle, (1, 0, 2)))


def with_halo(cells, sides, width):
    for axis, dim in sides:
        count = lax.axis_size(axis)
        ends = count - 1
        head = lax.slice_in_dim(cells, 0, width, axis=dim)
        tail = lax.slice_in_dim(cells, cells.shape[dim] - width, cells.shape[dim], axis=dim)
        cells = jnp.concatenate(
            [
                lax.ppermute(tail, axis, [(i, (i + 1) % count) for i in range(ends)]),
                cells,
                lax.ppermute(head, axis, [((i + 1) % count, i) for i in range(ends)]),
            ],
            axis=dim,
        )
    return cells


def silu_slope(values):
    sig = jax.nn.sigmoid(values)
    return sig * (1.0 + values * (1.0 - sig))


def conv_forward(padded, weight, extent):
    size_z, size_x, size_y = extent
    count_cells = size_z * size_x * size_y
    summed = jnp.zeros((count_cells, weight.shape[2]), jnp.float32)
    for tap_index in range(27):
        shift_z, shift_x, shift_y = (tap_index // 9, tap_index // 3 % 3, tap_index % 3)
        window = padded[
            shift_z : shift_z + size_z, shift_x : shift_x + size_x, shift_y : shift_y + size_y, :
        ]
        window = window.reshape(count_cells, padded.shape[3])
        summed = summed + jnp.dot(
            window, weight[:, tap_index, :], preferred_element_type=jnp.float32
        )
    return summed.reshape(size_z, size_x, size_y, weight.shape[2])


def conv_weight_grad(padded, gradient, extent):
    size_z, size_x, size_y = extent
    count_cells = size_z * size_x * size_y
    flat_gradient = gradient.reshape(count_cells, gradient.shape[3])
    pieces = []
    for tap_index in range(27):
        shift_z, shift_x, shift_y = (tap_index // 9, tap_index // 3 % 3, tap_index % 3)
        window = padded[
            shift_z : shift_z + size_z, shift_x : shift_x + size_x, shift_y : shift_y + size_y, :
        ]
        window = window.reshape(count_cells, padded.shape[3])
        pieces.append(
            lax.dot_general(
                window, flat_gradient, (((0,), (0,)), ((), ())), preferred_element_type=jnp.float32
            )
        )
    return jnp.stack(pieces, axis=1)


def conv_input_grad(padded, weight, extent):
    size_z, size_x, size_y = extent
    count_cells = size_z * size_x * size_y
    summed = jnp.zeros((count_cells, weight.shape[0]), jnp.float32)
    for tap_index in range(27):
        shift_z, shift_x, shift_y = (2 - tap_index // 9, 2 - tap_index // 3 % 3, 2 - tap_index % 3)
        window = padded[
            shift_z : shift_z + size_z, shift_x : shift_x + size_x, shift_y : shift_y + size_y, :
        ]
        window = window.reshape(count_cells, padded.shape[3])
        summed = summed + lax.dot_general(
            window,
            weight[:, tap_index, :],
            (((1,), (1,)), ((), ())),
            preferred_element_type=jnp.float32,
        )
    return summed.reshape(size_z, size_x, size_y, weight.shape[0])


def pool_features(fine, kernel):
    size_z, size_x, size_y, channels = fine.shape
    blocks = fine.reshape(size_z // 2, 2, size_x // 2, 2, size_y // 2, 2, channels)
    kernel_cube = kernel.reshape(2, 2, 2, kernel.shape[1], kernel.shape[2])
    return jnp.einsum(
        "zaxbycf,abcfg->zxyg", blocks, kernel_cube, preferred_element_type=jnp.float32
    )


def pool_adjoint(coarse_in, kernel):
    size_z, size_x, size_y, wide_channels = coarse_in.shape
    kernel_cube = kernel.reshape(2, 2, 2, kernel.shape[1], kernel.shape[2])
    result = jnp.einsum(
        "zxyg,abcfg->zaxbycf", coarse_in, kernel_cube, preferred_element_type=jnp.float32
    )
    return result.reshape(2 * size_z, 2 * size_x, 2 * size_y, kernel.shape[1])


def lift_features(coarse_in, kernel):
    size_z, size_x, size_y, wide_channels = coarse_in.shape
    kernel_cube = kernel.reshape(2, 2, 2, kernel.shape[1], kernel.shape[2])
    result = jnp.einsum(
        "zxyg,abcgf->zaxbycf", coarse_in, kernel_cube, preferred_element_type=jnp.float32
    )
    return result.reshape(2 * size_z, 2 * size_x, 2 * size_y, kernel.shape[2])


def lift_adjoint(fine, kernel):
    size_z, size_x, size_y, channels = fine.shape
    blocks = fine.reshape(size_z // 2, 2, size_x // 2, 2, size_y // 2, 2, channels)
    kernel_cube = kernel.reshape(2, 2, 2, kernel.shape[1], kernel.shape[2])
    return jnp.einsum(
        "zaxbycf,abcgf->zxyg", blocks, kernel_cube, preferred_element_type=jnp.float32
    )


def column_body(volume, cotangent, w_conv, w_down, w_bottle, w_up):
    size_z, size_x, size_y, channels = volume.shape
    group_channels = w_bottle.shape[2]
    half_x = size_x // 2
    half_y = size_y // 2
    padded = with_halo(volume, (("gx", 1), ("gy", 2), ("gz", 0)), 1)
    pre_hidden = conv_forward(padded, w_conv, (size_z, size_x, size_y))
    hidden = jax.nn.silu(pre_hidden).astype(jnp.bfloat16)
    hidden_slope = silu_slope(pre_hidden)
    coarse = pool_features(hidden, w_down).astype(jnp.bfloat16)
    stacked = lax.all_gather(coarse, "gz", axis=0, tiled=True)
    rimmed = with_halo(stacked, (("gx", 1), ("gy", 2)), 1)
    column_z = rimmed.shape[0]
    coarse_pad = jnp.pad(rimmed, ((1, 1), (0, 0), (0, 0), (0, 0)))
    pre_bottle = conv_forward(coarse_pad, w_bottle, (column_z, half_x, half_y))
    bottle = jax.nn.silu(pre_bottle).astype(jnp.bfloat16)
    bottle_slope = silu_slope(pre_bottle)
    own_start = lax.axis_index("gz") * group_channels
    own_up = lax.dynamic_slice_in_dim(w_up, own_start, group_channels, 1)
    lifted = lax.psum_scatter(
        lift_features(bottle, own_up).astype(jnp.bfloat16), "gz", scatter_dimension=0, tiled=True
    ).astype(jnp.float32)
    output = (lifted + hidden.astype(jnp.float32)).astype(jnp.bfloat16)
    back_bottle = lift_adjoint(cotangent, w_up).astype(jnp.bfloat16)
    split_grad = lax.all_to_all(back_bottle, "gz", split_axis=3, concat_axis=0, tiled=True)
    bottle_grad = (split_grad.astype(jnp.float32) * bottle_slope).astype(jnp.bfloat16)
    grad_bottle = lax.psum_scatter(
        conv_weight_grad(coarse_pad, bottle_grad, (column_z, half_x, half_y)),
        ("gx", "gy"),
        scatter_dimension=0,
        tiled=True,
    )
    grad_rimmed = with_halo(bottle_grad, (("gx", 1), ("gy", 2)), 1)
    grad_pad = jnp.pad(grad_rimmed, ((1, 1), (0, 0), (0, 0), (0, 0)))
    coarse_grad = lax.psum_scatter(
        conv_input_grad(
            grad_pad, w_bottle, (lax.axis_size("gz") * (size_z // 2), half_x, half_y)
        ).astype(jnp.bfloat16),
        "gz",
        scatter_dimension=0,
        tiled=True,
    )
    hidden_grad = (
        (pool_adjoint(coarse_grad, w_down) + cotangent.astype(jnp.float32)) * hidden_slope
    ).astype(jnp.bfloat16)
    full_term = conv_weight_grad(padded, hidden_grad, (size_z, size_x, size_y))
    depth_summed = lax.psum(full_term.astype(jnp.bfloat16), "gz").astype(jnp.float32)
    grad_conv = lax.psum_scatter(depth_summed, ("gx", "gy"), scatter_dimension=0, tiled=True)
    return (output, grad_conv, grad_bottle)


def fits_one_plane(counts, brick, wide):
    count_p = counts[0] * counts[1]
    size_z, size_x, size_y, channels = brick
    return (
        counts == (2, 4, 4)
        and count_p * (size_x // 2) * (size_y // 2) == 128
        and wide // count_p == 64
        and (size_z, size_x, size_y, channels) == (8, 8, 8, 128)
    )


def solution(mesh):
    in_specs = (
        P("gz", "gx", "gy", None),
        P("gz", "gx", "gy", None),
        P(),
        P(),
        P(None, None, "gz"),
        P(),
    )
    out_specs = (
        P("gz", "gx", "gy", None),
        P(("gx", "gy"), None, None),
        P(("gx", "gy"), None, "gz"),
    )
    counts = (mesh.shape["gx"], mesh.shape["gy"], mesh.shape["gz"])

    def body(volume, cotangent, w_conv, w_down, w_bottle, w_up):
        if fits_one_plane(counts, volume.shape, w_down.shape[2]):
            return gathered_body(counts, volume, cotangent, w_conv, w_down, w_bottle, w_up)
        return column_body(volume, cotangent, w_conv, w_down, w_bottle, w_up)

    return jax.shard_map(body, mesh=mesh, in_specs=in_specs, out_specs=out_specs, check_vma=False)
```

profile of v0, /device:TPU:0, one launch (start us, length us, event | category | flops | bytes accessed | tf_op | source)
XLA Modules:
  0.0 86.5 jit_solution(13867191950660932924)
XLA Ops:
  1.5 3.1 %collective-permute-start = (bf16[8,8,128]{2,1,0:T(8,128)(2,1)S(1)}, bf16[8,8,128]{2,1,0:T(8,128)(2,1)S(1)}, u32[]{:S(2)}, u32[]{:S(2)}) collective-permute-start(bf16[8,8,128]{2,1,0:T(8,128)(2,1)S(1)} %get-tuple-element.60), channel_id=1, source_target_pairs={{0,1},{1,0},{2,3},{3,2},{4,5},{5,4},{6,7},{7,6},{8,9},{9,8},{10,11... | collective-permute-start | bytes 49160 | tf_op jit(solution)/shard_map/ppermute | solution.py:646
  6.4 3.0 %collective-permute-start.3 = (bf16[16,128]{1,0:T(8,128)(2,1)S(1)}, bf16[16,128]{1,0:T(8,128)(2,1)S(1)}, u32[]{:S(2)}, u32[]{:S(2)}) collective-permute-start(bf16[16,128]{1,0:T(8,128)(2,1)S(1)} %get-tuple-element.63), channel_id=1, source_target_pairs={{0,24},{4,28},{8,16},{12,20},{16,8},{20,12},{24,0},{28,4},{1,25},{... | collective-permute-start | bytes 12296 | tf_op jit(solution)/shard_map/ppermute | solution.py:136
  11.0 2.8 %collective-permute-done.4.across = bf16[80,128]{1,0:T(8,128)(2,1)S(1)} collective-permute-done((bf16[80,128]{1,0:T(8,128)(2,1)S(1)}, bf16[80,128]{1,0:T(8,128)(2,1)S(1)}, u32[]{:S(2)}, u32[]{:S(2)}) %collective-permute-start.4) | collective-permute-done | bytes 20512 | tf_op jit(solution)/shard_map/ppermute | solution.py:136
  15.1 1.5 %hidden.1 = (bf16[8,64,128]{2,1,0:T(8,128)(2,1)S(1)}, f32[8,64,128]{2,1,0:T(8,128)S(1)}, bf16[10,128,128]{2,1,0:T(8,128)(2,1)S(1)}, bf16[64,640]{1,0:T(8,128)(2,...) custom-call(bf16[8,8,8,128]{3,2,1,0:T(8,128)(2,1)S(1)} %copy-done.10, ...), custom_call_target="tpu_custom_call" | custom-call | flops 2000000000 | bytes 2000000 | tf_op jit(solution)/shard_map/hidden/pallas_call | solution.py:18
  16.7 3.7 %collective-permute-start.6 = (bf16[64,640]{1,0:T(8,128)(2,1)S(1)}, bf16[64,640]{1,0:T(8,128)(2,1)S(1)}, u32[]{:S(2)}, u32[]{:S(2)}) collective-permute-start(bf16[64,640]{1,0:T(8,128)(2,1)S(1)} %get-tuple-element.71), channel_id=1, source_target_pairs={{0,3},{1,2},{2,1},{3,0},{4,7},{5,6},{6,5},{7,4},{8,11},{9,10},{10,... | collective-permute-start | bytes 245768 | tf_op jit(solution)/shard_map/ppermute | solution.py:136
  20.3 2.5 %collective-permute-start.7 = (bf16[64,640]{1,0:T(8,128)(2,1)S(1)}, bf16[64,640]{1,0:T(8,128)(2,1)S(1)}, u32[]{:S(2)}, u32[]{:S(2)}) collective-permute-start(bf16[64,640]{1,0:T(8,128)(2,1)S(1)} %get-tuple-element.72), channel_id=1, source_target_pairs={{0,2},{1,3},{2,0},{3,1},{4,6},{5,7},{6,4},{7,5},{8,10},{9,11},{10,... | collective-permute-start | bytes 245768 | tf_op jit(solution)/shard_map/ppermute | solution.py:136
  23.3 5.7 %collective-permute-done.7.refs_2_ = bf16[64,640]{1,0:T(8,128)(2,1)S(1)} collective-permute-done((bf16[64,640]{1,0:T(8,128)(2,1)S(1)}, bf16[64,640]{1,0:T(8,128)(2,1)S(1)}, u32[]{:S(2)}, u32[]{:S(2)}) %collective-permute-start.7) | collective-permute-done | bytes 81952 | tf_op jit(solution)/shard_map/ppermute | solution.py:136
  29.3 1.6 %collective-permute-start.10 = (bf16[16,512]{1,0:T(8,128)(2,1)S(1)}, bf16[16,512]{1,0:T(8,128)(2,1)S(1)}, u32[]{:S(2)}, u32[]{:S(2)}) collective-permute-start(bf16[16,512]{1,0:T(8,128)(2,1)S(1)} %get-tuple-element.82), channel_id=1, source_target_pairs={{0,24},{4,28},{8,16},{12,20},{16,8},{20,12},{24,0},{28,4},{1,25},{... | collective-permute-start | bytes 49160 | tf_op jit(solution)/shard_map/ppermute | solution.py:136
  31.4 1.5 %collective-permute-start.11 = (bf16[64,512]{1,0:T(8,128)(2,1)S(1)}, bf16[64,512]{1,0:T(8,128)(2,1)S(1)}, u32[]{:S(2)}, u32[]{:S(2)}) collective-permute-start(bf16[64,512]{1,0:T(8,128)(2,1)S(1)} %get-tuple-element.83), channel_id=1, source_target_pairs={{0,8},{4,12},{8,0},{12,4},{16,24},{20,28},{24,16},{28,20},{1,9},{5... | collective-permute-start | bytes 196616 | tf_op jit(solution)/shard_map/ppermute | solution.py:136
  32.9 1.3 %collective-permute-done.10.block = bf16[16,512]{1,0:T(8,128)(2,1)S(1)} collective-permute-done((bf16[16,512]{1,0:T(8,128)(2,1)S(1)}, bf16[16,512]{1,0:T(8,128)(2,1)S(1)}, u32[]{:S(2)}, u32[]{:S(2)}) %collective-permute-start.10) | collective-permute-done | bytes 16416 | tf_op jit(solution)/shard_map/ppermute | solution.py:136
  35.9 1.2 %collective-permute-done.12.refs_3_ = bf16[160,512]{1,0:T(8,128)(2,1)S(1)} collective-permute-done((bf16[160,512]{1,0:T(8,128)(2,1)S(1)}, bf16[160,512]{1,0:T(8,128)(2,1)S(1)}, u32[]{:S(2)}, u32[]{:S(2)}) %collective-permute-start.12) | collective-permute-done | bytes 163872 | tf_op jit(solution)/shard_map/ppermute | solution.py:136
  37.1 2.1 %bottle.1 = (bf16[256,128]{1,0:T(8,128)(2,1)S(1)}, bf16[512,128]{1,0:T(8,128)(2,1)S(1)}, bf16[512,128]{1,0:T(8,128)(2,1)S(1)}, bf16[512,128]{1,0:T(8,128)(2,1)S(1)}, bf16[512,128]{1,0:T(8,128)(2,1)S(1)}) custom-call(bf16[256,512]{1,0:T(8,128)(2,1)S(1)} %get-tuple-element.79.refs_0_, bf16[256,128]{1,0:T(8,128)(2,1)S(1)} %get-tuple-element.80.refs_1_, ...), custom_call_target="tpu_custom_call" | custom-call | flops 2000000000 | bytes 2000000 | tf_op jit(solution)/shard_map/bottle/pallas_call | solution.py:18
  39.2 2.5 %collective-permute-start.13 = (bf16[512,128]{1,0:T(8,128)(2,1)S(1)}, bf16[512,128]{1,0:T(8,128)(2,1)S(1)}, u32[]{:S(2)}, u32[]{:S(2)}) collective-permute-start(bf16[512,128]{1,0:T(8,128)(2,1)S(1)} %get-tuple-element.90), channel_id=1, source_target_pairs={{0,24},{4,28},{8,16},{12,20},{16,8},{20,12},{24,0},{28,4},{1,25},{... | collective-permute-start | bytes 393224 | tf_op jit(solution)/shard_map/ppermute | solution.py:136
  42.8 3.2 %collective-permute-done.13.refs_2_.refs_7_.refs_6_ = bf16[512,128]{1,0:T(8,128)(2,1)S(1)} collective-permute-done((bf16[512,128]{1,0:T(8,128)(2,1)S(1)}, bf16[512,128]{1,0:T(8,128)(2,1)S(1)}, u32[]{:S(2)}, u32[]{:S(2)}) %collective-permute-start.13) | collective-permute-done | bytes 131104 | tf_op jit(solution)/shard_map/ppermute | solution.py:136
  46.0 2.5 %collective-permute-done.15.refs_4_.refs_5_ = bf16[512,128]{1,0:T(8,128)(2,1)S(1)} collective-permute-done((bf16[512,128]{1,0:T(8,128)(2,1)S(1)}, bf16[512,128]{1,0:T(8,128)(2,1)S(1)}, u32[]{:S(2)}, u32[]{:S(2)}) %collective-permute-start.15) | collective-permute-done | bytes 131104 | tf_op jit(solution)/shard_map/ppermute | solution.py:136
  50.1 1.6 %coarse_grad.1 = (bf16[64,640]{1,0:T(8,128)(2,1)S(1)}, bf16[64,640]{1,0:T(8,128)(2,1)S(1)}, bf16[64,640]{1,0:T(8,128)(2,1)S(1)}, bf16[64,640]{1,0:T(8,128)(2,1)S(1)}) custom-call(bf16[512,128]{1,0:T(8,128)(2,1)S(1)} %get-tuple-element.102.refs_0_.refs_1_, bf16[512,128]{1,0:T(8,128)(2,1)S(1)} %collective-permute-done.14.refs_1_.refs_8_.refs_7_, ...), custom_call_target="tpu_custom_call" | custom-call | flops 300000000 | bytes 300000 | tf_op jit(solution)/shard_map/coarse_grad/pallas_call | solution.py:18
  51.7 2.9 %collective-permute-start.20 = (bf16[64,640]{1,0:T(8,128)(2,1)S(1)}, bf16[64,640]{1,0:T(8,128)(2,1)S(1)}, u32[]{:S(2)}, u32[]{:S(2)}) collective-permute-start(bf16[64,640]{1,0:T(8,128)(2,1)S(1)} %get-tuple-element.95), channel_id=1, source_target_pairs={{0,3},{1,2},{2,1},{3,0},{4,7},{5,6},{6,5},{7,4},{8,11},{9,10},{10,... | collective-permute-start | bytes 245768 | tf_op jit(solution)/shard_map/ppermute | solution.py:136
  54.6 1.5 %collective-permute-start.22 = (bf16[64,640]{1,0:T(8,128)(2,1)S(1)}, bf16[64,640]{1,0:T(8,128)(2,1)S(1)}, u32[]{:S(2)}, u32[]{:S(2)}) collective-permute-start(bf16[64,640]{1,0:T(8,128)(2,1)S(1)} %get-tuple-element.97), channel_id=1, source_target_pairs={{0,1},{1,0},{2,3},{3,2},{4,5},{5,4},{6,7},{7,6},{8,9},{9,8},{10,11... | collective-permute-start | bytes 245768 | tf_op jit(solution)/shard_map/ppermute | solution.py:136
  57.8 1.1 %collective-permute-done.20.refs_1_ = bf16[64,640]{1,0:T(8,128)(2,1)S(1)} collective-permute-done((bf16[64,640]{1,0:T(8,128)(2,1)S(1)}, bf16[64,640]{1,0:T(8,128)(2,1)S(1)}, u32[]{:S(2)}, u32[]{:S(2)}) %collective-permute-start.20) | collective-permute-done | bytes 81952 | tf_op jit(solution)/shard_map/ppermute | solution.py:136
  58.9 2.9 %collective-permute-done.21.refs_2_ = bf16[64,640]{1,0:T(8,128)(2,1)S(1)} collective-permute-done((bf16[64,640]{1,0:T(8,128)(2,1)S(1)}, bf16[64,640]{1,0:T(8,128)(2,1)S(1)}, u32[]{:S(2)}, u32[]{:S(2)}) %collective-permute-start.21) | collective-permute-done | bytes 81952 | tf_op jit(solution)/shard_map/ppermute | solution.py:136
  61.7 1.1 %hidden_grad.1 = (bf16[640,384]{1,0:T(8,128)(2,1)S(1)}, bf16[64,512]{1,0:T(8,128)(2,1)S(1)}, bf16[4,432,128]{2,1,0:T(8,128)(2,1)S(1)}) custom-call(bf16[64,640]{1,0:T(8,128)(2,1)S(1)} %get-tuple-element.94.refs_0_, bf16[64,640]{1,0:T(8,128)(2,1)S(1)} %collective-permute-done.20.refs_1_, bf16[64,640]{1,0:T(8,128)(2,1)S(1)} %collective-permute-done.21.refs_2_, ...), custom_call_target="tpu_custom_call" | custom-call | flops 300000000 | bytes 300000 | tf_op jit(solution)/shard_map/hidden_grad/pallas_call | solution.py:18
  63.5 1.2 %collective-permute-done.23.got = bf16[4,432,128]{2,1,0:T(8,128)(2,1)S(1)} collective-permute-done((bf16[4,432,128]{2,1,0:T(8,128)(2,1)S(1)}, bf16[4,432,128]{2,1,0:T(8,128)(2,1)S(1)}, u32[]{:S(2)}, u32[]{:S(2)}) %collective-permute-start.23) | collective-permute-done | bytes 442400 | tf_op jit(solution)/shard_map/ppermute | solution.py:136
  64.8 1.8 %collective-permute-start.24 = (bf16[432,128]{1,0:T(8,128)(2,1)S(1)}, bf16[432,128]{1,0:T(8,128)(2,1)S(1)}, u32[]{:S(2)}, u32[]{:S(2)}) collective-permute-start(bf16[432,128]{1,0:T(8,128)(2,1)S(1)} %get-tuple-element.107), channel_id=1, source_target_pairs={{0,24},{4,28},{8,16},{12,20},{16,8},{20,12},{24,0},{28,4},{1,25},{... | collective-permute-start | bytes 331784 | tf_op jit(solution)/shard_map/ppermute | solution.py:136
  66.6 1.2 %collective-permute-start.25 = (bf16[432,128]{1,0:T(8,128)(2,1)S(1)}, bf16[432,128]{1,0:T(8,128)(2,1)S(1)}, u32[]{:S(2)}, u32[]{:S(2)}) collective-permute-start(bf16[432,128]{1,0:T(8,128)(2,1)S(1)} %get-tuple-element.108), channel_id=1, source_target_pairs={{0,16},{4,20},{8,24},{12,28},{16,0},{20,4},{24,8},{28,12},{1,17},{... | collective-permute-start | bytes 331784 | tf_op jit(solution)/shard_map/ppermute | solution.py:136
  68.4 1.1 %output.1 = bf16[8,8,8,128]{3,2,1,0:T(8,128)(2,1)} custom-call(bf16[64,512]{1,0:T(8,128)(2,1)S(1)} %get-tuple-element.110.bottle, bf16[8,64,128]{2,1,0:T(8,128)(2,1)S(1)} %get-tuple-element.111.hidden, bf16[8,512,128]{2,1,0:T(8,128)(2,1)S(1)} %copy-done, bf16[64,64]{1,0:T(8,128)(2,1)S(1)} %copy-done.6), custom_call_target="tpu_custom_call" | custom-call | flops 300000000 | bytes 300000 | tf_op jit(solution)/shard_map/output/pallas_call | solution.py:18
  69.5 2.0 %collective-permute-done.24.refs_1_ = bf16[432,128]{1,0:T(8,128)(2,1)S(1)} collective-permute-done((bf16[432,128]{1,0:T(8,128)(2,1)S(1)}, bf16[432,128]{1,0:T(8,128)(2,1)S(1)}, u32[]{:S(2)}, u32[]{:S(2)}) %collective-permute-start.24) | collective-permute-done | bytes 110624 | tf_op jit(solution)/shard_map/ppermute | solution.py:136
  71.5 1.7 %collective-permute-done.25.refs_2_ = bf16[432,128]{1,0:T(8,128)(2,1)S(1)} collective-permute-done((bf16[432,128]{1,0:T(8,128)(2,1)S(1)}, bf16[432,128]{1,0:T(8,128)(2,1)S(1)}, u32[]{:S(2)}, u32[]{:S(2)}) %collective-permute-start.25) | collective-permute-done | bytes 110624 | tf_op jit(solution)/shard_map/ppermute | solution.py:136
  73.4 1.2 %collective-permute-start.27 = (bf16[432,128]{1,0:T(8,128)(2,1)S(1)}, bf16[432,128]{1,0:T(8,128)(2,1)S(1)}, u32[]{:S(2)}, u32[]{:S(2)}) collective-permute-start(bf16[432,128]{1,0:T(8,128)(2,1)S(1)} %plane_sum.1.refs_0_), channel_id=1, source_target_pairs={{0,1},{1,0},{2,3},{3,2},{4,5},{5,4},{6,7},{7,6},{8,9},{9,8},{10,11... | collective-permute-start | bytes 331784 | tf_op jit(solution)/shard_map/ppermute | solution.py:136
  74.8 3.6 %collective-permute-done.27.refs_1_ = bf16[432,128]{1,0:T(8,128)(2,1)S(1)} collective-permute-done((bf16[432,128]{1,0:T(8,128)(2,1)S(1)}, bf16[432,128]{1,0:T(8,128)(2,1)S(1)}, u32[]{:S(2)}, u32[]{:S(2)}) %collective-permute-start.27) | collective-permute-done | bytes 110624 | tf_op jit(solution)/shard_map/ppermute | solution.py:136
  78.4 1.5 %collective-permute-start.28 = (bf16[432,128]{1,0:T(8,128)(2,1)S(1)}, bf16[432,128]{1,0:T(8,128)(2,1)S(1)}, u32[]{:S(2)}, u32[]{:S(2)}) collective-permute-start(bf16[432,128]{1,0:T(8,128)(2,1)S(1)} %depth_sum.1.refs_0_), channel_id=1, source_target_pairs={{0,2},{1,3},{2,0},{3,1},{4,6},{5,7},{6,4},{7,5},{8,10},{9,11},{10,... | collective-permute-start | bytes 331784 | tf_op jit(solution)/shard_map/ppermute | solution.py:136
  79.9 2.9 %grad_bottle.1 = f32[27,64,128]{2,1,0:T(8,128)} custom-call(bf16[1152,1024]{1,0:T(8,128)(2,1)S(1)} %coarse_transpose.1.turned, bf16[1024,640]{1,0:T(8,128)(2,1)S(1)} %wide.1), custom_call_target="tpu_custom_call" | custom-call | flops 4000000000 | bytes 4000000 | tf_op jit(solution)/shard_map/grad_bottle/pallas_call | solution.py:18
  82.8 2.9 %collective-permute-done.28.refs_1_ = bf16[432,128]{1,0:T(8,128)(2,1)S(1)} collective-permute-done((bf16[432,128]{1,0:T(8,128)(2,1)S(1)}, bf16[432,128]{1,0:T(8,128)(2,1)S(1)}, u32[]{:S(2)}, u32[]{:S(2)}) %collective-permute-start.28) | collective-permute-done | bytes 110624 | tf_op jit(solution)/shard_map/ppermute | solution.py:136
  (77 shorter events, 15.2 us)
Async XLA Ops:
  1.5 4.8 %collective-permute-start = (bf16[8,8,128]{2,1,0:T(8,128)(2,1)S(1)}, bf16[8,8,128]{2,1,0:T(8,128)(2,1)S(1)}, u32[]{:S(2)}, u32[]{:S(2)}) collective-permute-start(bf16[8,8,128]{2,1,0:T(8,128)(2,1)S(1)} %get-tuple-element.60), channel_id=1, source_target_pairs={{0,1},{1,0},{2,3},{3,2},{4,5},{5,4},{6,7},{7,6},{8,9},{9,8},{10,11... | collective-permute-start | bytes 49160 | tf_op jit(solution)/shard_map/ppermute | solution.py:646
  4.6 1.7 %collective-permute-start.1 = (bf16[8,8,128]{2,1,0:T(8,128)(2,1)S(1)}, bf16[8,8,128]{2,1,0:T(8,128)(2,1)S(1)}, u32[]{:S(2)}, u32[]{:S(2)}) collective-permute-start(bf16[8,8,128]{2,1,0:T(8,128)(2,1)S(1)} %get-tuple-element.61), channel_id=1, source_target_pairs={{1,2},{2,1},{5,6},{6,5},{9,10},{10,9},{13,14},{14,13},{17,18},{18,... | collective-permute-start | bytes 49160 | tf_op jit(solution)/shard_map/ppermute | solution.py:645
  6.4 4.6 %collective-permute-start.3 = (bf16[16,128]{1,0:T(8,128)(2,1)S(1)}, bf16[16,128]{1,0:T(8,128)(2,1)S(1)}, u32[]{:S(2)}, u32[]{:S(2)}) collective-permute-start(bf16[16,128]{1,0:T(8,128)(2,1)S(1)} %get-tuple-element.63), channel_id=1, source_target_pairs={{0,24},{4,28},{8,16},{12,20},{16,8},{20,12},{24,0},{28,4},{1,25},{... | collective-permute-start | bytes 12296 | tf_op jit(solution)/shard_map/ppermute | solution.py:136
  9.4 4.4 %collective-permute-start.2 = (bf16[128,128]{1,0:T(8,128)(2,1)S(1)}, bf16[128,128]{1,0:T(8,128)(2,1)S(1)}, u32[]{:S(2)}, u32[]{:S(2)}) collective-permute-start(bf16[128,128]{1,0:T(8,128)(2,1)S(1)} %get-tuple-element.62), channel_id=1, source_target_pairs={{0,16},{4,20},{8,24},{12,28},{16,0},{20,4},{24,8},{28,12},{1,17},{... | collective-permute-start | bytes 98312 | tf_op jit(solution)/shard_map/ppermute | solution.py:136
  9.9 3.8 %collective-permute-start.4 = (bf16[80,128]{1,0:T(8,128)(2,1)S(1)}, bf16[80,128]{1,0:T(8,128)(2,1)S(1)}, u32[]{:S(2)}, u32[]{:S(2)}) collective-permute-start(bf16[80,128]{1,0:T(8,128)(2,1)S(1)} %get-tuple-element.64), channel_id=1, source_target_pairs={{0,8},{4,12},{8,0},{12,4},{16,24},{20,28},{24,16},{28,20},{1,9},{5... | collective-permute-start | bytes 61448 | tf_op jit(solution)/shard_map/ppermute | solution.py:136
  13.8 1.3 %collective-permute-start.5 = (bf16[192,128]{1,0:T(8,128)(2,1)S(1)}, bf16[192,128]{1,0:T(8,128)(2,1)S(1)}, u32[]{:S(2)}, u32[]{:S(2)}) collective-permute-start(bf16[192,128]{1,0:T(8,128)(2,1)S(1)} %relay_rims.2), channel_id=1, source_target_pairs={{0,4},{4,0},{8,12},{12,8},{16,20},{20,16},{24,28},{28,24},{1,5},{5... | collective-permute-start | bytes 147464 | tf_op jit(solution)/shard_map/ppermute | solution.py:136
  15.1 13.9 %copy-start.12 = (bf16[2,224,256]{2,1,0:T(8,128)(2,1)S(1)}, bf16[2,224,256]{2,1,0:T(8,128)(2,1)}, u32[]{:S(2)}) copy-start(bf16[2,224,256]{2,1,0:T(8,128)(2,1)} %constant.19.clone.refs_4_) | copy-start | bytes 688132
  16.7 6.7 %collective-permute-start.6 = (bf16[64,640]{1,0:T(8,128)(2,1)S(1)}, bf16[64,640]{1,0:T(8,128)(2,1)S(1)}, u32[]{:S(2)}, u32[]{:S(2)}) collective-permute-start(bf16[64,640]{1,0:T(8,128)(2,1)S(1)} %get-tuple-element.71), channel_id=1, source_target_pairs={{0,3},{1,2},{2,1},{3,0},{4,7},{5,6},{6,5},{7,4},{8,11},{9,10},{10,... | collective-permute-start | bytes 245768 | tf_op jit(solution)/shard_map/ppermute | solution.py:136
  20.3 8.7 %collective-permute-start.7 = (bf16[64,640]{1,0:T(8,128)(2,1)S(1)}, bf16[64,640]{1,0:T(8,128)(2,1)S(1)}, u32[]{:S(2)}, u32[]{:S(2)}) collective-permute-start(bf16[64,640]{1,0:T(8,128)(2,1)S(1)} %get-tuple-element.72), channel_id=1, source_target_pairs={{0,2},{1,3},{2,0},{3,1},{4,6},{5,7},{6,4},{7,5},{8,10},{9,11},{10,... | collective-permute-start | bytes 245768 | tf_op jit(solution)/shard_map/ppermute | solution.py:136
  22.9 6.2 %collective-permute-start.8 = (bf16[64,640]{1,0:T(8,128)(2,1)S(1)}, bf16[64,640]{1,0:T(8,128)(2,1)S(1)}, u32[]{:S(2)}, u32[]{:S(2)}) collective-permute-start(bf16[64,640]{1,0:T(8,128)(2,1)S(1)} %get-tuple-element.73), channel_id=1, source_target_pairs={{0,1},{1,0},{2,3},{3,2},{4,5},{5,4},{6,7},{7,6},{8,9},{9,8},{10,11... | collective-permute-start | bytes 245768 | tf_op jit(solution)/shard_map/ppermute | solution.py:136
  29.3 4.9 %collective-permute-start.10 = (bf16[16,512]{1,0:T(8,128)(2,1)S(1)}, bf16[16,512]{1,0:T(8,128)(2,1)S(1)}, u32[]{:S(2)}, u32[]{:S(2)}) collective-permute-start(bf16[16,512]{1,0:T(8,128)(2,1)S(1)} %get-tuple-element.82), channel_id=1, source_target_pairs={{0,24},{4,28},{8,16},{12,20},{16,8},{20,12},{24,0},{28,4},{1,25},{... | collective-permute-start | bytes 49160 | tf_op jit(solution)/shard_map/ppermute | solution.py:136
  30.9 4.3 %collective-permute-start.9 = (bf16[64,512]{1,0:T(8,128)(2,1)S(1)}, bf16[64,512]{1,0:T(8,128)(2,1)S(1)}, u32[]{:S(2)}, u32[]{:S(2)}) collective-permute-start(bf16[64,512]{1,0:T(8,128)(2,1)S(1)} %get-tuple-element.81), channel_id=1, source_target_pairs={{0,16},{4,20},{8,24},{12,28},{16,0},{20,4},{24,8},{28,12},{1,17},{... | collective-permute-start | bytes 196616 | tf_op jit(solution)/shard_map/ppermute | solution.py:136
  31.4 4.3 %collective-permute-start.11 = (bf16[64,512]{1,0:T(8,128)(2,1)S(1)}, bf16[64,512]{1,0:T(8,128)(2,1)S(1)}, u32[]{:S(2)}, u32[]{:S(2)}) collective-permute-start(bf16[64,512]{1,0:T(8,128)(2,1)S(1)} %get-tuple-element.83), channel_id=1, source_target_pairs={{0,8},{4,12},{8,0},{12,4},{16,24},{20,28},{24,16},{28,20},{1,9},{5... | collective-permute-start | bytes 196616 | tf_op jit(solution)/shard_map/ppermute | solution.py:136
  35.7 1.5 %collective-permute-start.12 = (bf16[160,512]{1,0:T(8,128)(2,1)S(1)}, bf16[160,512]{1,0:T(8,128)(2,1)S(1)}, u32[]{:S(2)}, u32[]{:S(2)}) collective-permute-start(bf16[160,512]{1,0:T(8,128)(2,1)S(1)} %relay_rims.3), channel_id=1, source_target_pairs={{0,4},{4,0},{8,12},{12,8},{16,20},{20,16},{24,28},{28,24},{1,5},{5... | collective-permute-start | bytes 491528 | tf_op jit(solution)/shard_map/ppermute | solution.py:136
  37.1 12.9 %copy-start.2 = (bf16[1152,128]{1,0:T(8,128)(2,1)S(1)}, bf16[1152,128]{1,0:T(8,128)(2,1)}, u32[]{:S(2)}) copy-start(bf16[1152,128]{1,0:T(8,128)(2,1)} %constant.18.clone.refs_9_.refs_0_) | copy-start | bytes 884740
  39.2 6.8 %collective-permute-start.13 = (bf16[512,128]{1,0:T(8,128)(2,1)S(1)}, bf16[512,128]{1,0:T(8,128)(2,1)S(1)}, u32[]{:S(2)}, u32[]{:S(2)}) collective-permute-start(bf16[512,128]{1,0:T(8,128)(2,1)S(1)} %get-tuple-element.90), channel_id=1, source_target_pairs={{0,24},{4,28},{8,16},{12,20},{16,8},{20,12},{24,0},{28,4},{1,25},{... | collective-permute-start | bytes 393224 | tf_op jit(solution)/shard_map/ppermute | solution.py:136
  41.7 6.8 %collective-permute-start.15 = (bf16[512,128]{1,0:T(8,128)(2,1)S(1)}, bf16[512,128]{1,0:T(8,128)(2,1)S(1)}, u32[]{:S(2)}, u32[]{:S(2)}) collective-permute-start(bf16[512,128]{1,0:T(8,128)(2,1)S(1)} %get-tuple-element.91), channel_id=1, source_target_pairs={{0,16},{4,20},{8,24},{12,28},{16,0},{20,4},{24,8},{28,12},{1,17},{... | collective-permute-start | bytes 393224 | tf_op jit(solution)/shard_map/ppermute | solution.py:136
  42.2 6.4 %collective-permute-start.17 = (bf16[512,128]{1,0:T(8,128)(2,1)S(1)}, bf16[512,128]{1,0:T(8,128)(2,1)S(1)}, u32[]{:S(2)}, u32[]{:S(2)}) collective-permute-start(bf16[512,128]{1,0:T(8,128)(2,1)S(1)} %get-tuple-element.92), channel_id=1, source_target_pairs={{0,8},{4,12},{8,0},{12,4},{16,24},{20,28},{24,16},{28,20},{1,9},{5... | collective-permute-start | bytes 393224 | tf_op jit(solution)/shard_map/ppermute | solution.py:136
  42.8 6.3 %collective-permute-start.19 = (bf16[512,128]{1,0:T(8,128)(2,1)S(1)}, bf16[512,128]{1,0:T(8,128)(2,1)S(1)}, u32[]{:S(2)}, u32[]{:S(2)}) collective-permute-start(bf16[512,128]{1,0:T(8,128)(2,1)S(1)} %get-tuple-element.102.refs_0_.refs_1_), channel_id=1, source_target_pairs={{0,4},{4,0},{8,12},{12,8},{16,20},{20,16},{24,28},{28,24},{1,5},{5... | collective-permute-start | bytes 393224 | tf_op jit(solution)/shard_map/ppermute | solution.py:136
  46.0 3.0 %collective-permute-start.14 = (bf16[512,128]{1,0:T(8,128)(2,1)S(1)}, bf16[512,128]{1,0:T(8,128)(2,1)S(1)}, u32[]{:S(2)}, u32[]{:S(2)}) collective-permute-start(bf16[512,128]{1,0:T(8,128)(2,1)S(1)} %collective-permute-done.13.refs_2_.refs_7_.refs_6_), channel_id=1, source_target_pairs={{0,4},{4,0},{8,12},{12,8},{16,20},{20,16},{24,28},{28,24},{1,5},{5... | collective-permute-start | bytes 393224 | tf_op jit(solution)/shard_map/ppermute | solution.py:136
  48.5 1.3 %collective-permute-start.16 = (bf16[512,128]{1,0:T(8,128)(2,1)S(1)}, bf16[512,128]{1,0:T(8,128)(2,1)S(1)}, u32[]{:S(2)}, u32[]{:S(2)}) collective-permute-start(bf16[512,128]{1,0:T(8,128)(2,1)S(1)} %collective-permute-done.15.refs_4_.refs_5_), channel_id=1, source_target_pairs={{0,4},{4,0},{8,12},{12,8},{16,20},{20,16},{24,28},{28,24},{1,5},{5... | collective-permute-start | bytes 393224 | tf_op jit(solution)/shard_map/ppermute | solution.py:136
  48.6 1.4 %collective-permute-start.18 = (bf16[512,128]{1,0:T(8,128)(2,1)S(1)}, bf16[512,128]{1,0:T(8,128)(2,1)S(1)}, u32[]{:S(2)}, u32[]{:S(2)}) collective-permute-start(bf16[512,128]{1,0:T(8,128)(2,1)S(1)} %collective-permute-done.17.refs_6_.refs_3_.refs_2_), channel_id=1, source_target_pairs={{0,4},{4,0},{8,12},{12,8},{16,20},{20,16},{24,28},{28,24},{1,5},{5... | collective-permute-start | bytes 393224 | tf_op jit(solution)/shard_map/ppermute | solution.py:136
  50.1 6.1 %copy-start.4 = (bf16[256,1152]{1,0:T(8,128)(2,1)S(1)}, bf16[256,1152]{1,0:T(8,128)(2,1)}, u32[]{:S(2)}) copy-start(bf16[256,1152]{1,0:T(8,128)(2,1)} %constant.17.clone.refs_1_) | copy-start | bytes 1769476
  51.7 7.2 %collective-permute-start.20 = (bf16[64,640]{1,0:T(8,128)(2,1)S(1)}, bf16[64,640]{1,0:T(8,128)(2,1)S(1)}, u32[]{:S(2)}, u32[]{:S(2)}) collective-permute-start(bf16[64,640]{1,0:T(8,128)(2,1)S(1)} %get-tuple-element.95), channel_id=1, source_target_pairs={{0,3},{1,2},{2,1},{3,0},{4,7},{5,6},{6,5},{7,4},{8,11},{9,10},{10,... | collective-permute-start | bytes 245768 | tf_op jit(solution)/shard_map/ppermute | solution.py:136
  54.6 7.1 %collective-permute-start.21 = (bf16[64,640]{1,0:T(8,128)(2,1)S(1)}, bf16[64,640]{1,0:T(8,128)(2,1)S(1)}, u32[]{:S(2)}, u32[]{:S(2)}) collective-permute-start(bf16[64,640]{1,0:T(8,128)(2,1)S(1)} %get-tuple-element.96), channel_id=1, source_target_pairs={{0,2},{1,3},{2,0},{3,1},{4,6},{5,7},{6,4},{7,5},{8,10},{9,11},{10,... | collective-permute-start | bytes 245768 | tf_op jit(solution)/shard_map/ppermute | solution.py:136
  54.6 7.1 %collective-permute-start.22 = (bf16[64,640]{1,0:T(8,128)(2,1)S(1)}, bf16[64,640]{1,0:T(8,128)(2,1)S(1)}, u32[]{:S(2)}, u32[]{:S(2)}) collective-permute-start(bf16[64,640]{1,0:T(8,128)(2,1)S(1)} %get-tuple-element.97), channel_id=1, source_target_pairs={{0,1},{1,0},{2,3},{3,2},{4,5},{5,4},{6,7},{7,6},{8,9},{9,8},{10,11... | collective-permute-start | bytes 245768 | tf_op jit(solution)/shard_map/ppermute | solution.py:136
  62.9 1.9 %collective-permute-start.23 = (bf16[4,432,128]{2,1,0:T(8,128)(2,1)S(1)}, bf16[4,432,128]{2,1,0:T(8,128)(2,1)S(1)}, u32[]{:S(2)}, u32[]{:S(2)}) collective-permute-start(bf16[4,432,128]{2,1,0:T(8,128)(2,1)S(1)} %get-tuple-element.105), channel_id=1, source_target_pairs={{0,4},{4,0},{8,12},{12,8},{16,20},{20,16},{24,28},{28,24},{1,5},{5... | collective-permute-start | bytes 1327112 | tf_op jit(solution)/shard_map/ppermute | solution.py:136
  64.8 6.7 %collective-permute-start.24 = (bf16[432,128]{1,0:T(8,128)(2,1)S(1)}, bf16[432,128]{1,0:T(8,128)(2,1)S(1)}, u32[]{:S(2)}, u32[]{:S(2)}) collective-permute-start(bf16[432,128]{1,0:T(8,128)(2,1)S(1)} %get-tuple-element.107), channel_id=1, source_target_pairs={{0,24},{4,28},{8,16},{12,20},{16,8},{20,12},{24,0},{28,4},{1,25},{... | collective-permute-start | bytes 331784 | tf_op jit(solution)/shard_map/ppermute | solution.py:136
  66.6 6.6 %collective-permute-start.25 = (bf16[432,128]{1,0:T(8,128)(2,1)S(1)}, bf16[432,128]{1,0:T(8,128)(2,1)S(1)}, u32[]{:S(2)}, u32[]{:S(2)}) collective-permute-start(bf16[432,128]{1,0:T(8,128)(2,1)S(1)} %get-tuple-element.108), channel_id=1, source_target_pairs={{0,16},{4,20},{8,24},{12,28},{16,0},{20,4},{24,8},{28,12},{1,17},{... | collective-permute-start | bytes 331784 | tf_op jit(solution)/shard_map/ppermute | solution.py:136
  67.8 5.5 %collective-permute-start.26 = (bf16[432,128]{1,0:T(8,128)(2,1)S(1)}, bf16[432,128]{1,0:T(8,128)(2,1)S(1)}, u32[]{:S(2)}, u32[]{:S(2)}) collective-permute-start(bf16[432,128]{1,0:T(8,128)(2,1)S(1)} %get-tuple-element.109), channel_id=1, source_target_pairs={{0,8},{4,12},{8,0},{12,4},{16,24},{20,28},{24,16},{28,20},{1,9},{5... | collective-permute-start | bytes 331784 | tf_op jit(solution)/shard_map/ppermute | solution.py:136
  73.4 5.0 %collective-permute-start.27 = (bf16[432,128]{1,0:T(8,128)(2,1)S(1)}, bf16[432,128]{1,0:T(8,128)(2,1)S(1)}, u32[]{:S(2)}, u32[]{:S(2)}) collective-permute-start(bf16[432,128]{1,0:T(8,128)(2,1)S(1)} %plane_sum.1.refs_0_), channel_id=1, source_target_pairs={{0,1},{1,0},{2,3},{3,2},{4,5},{5,4},{6,7},{7,6},{8,9},{9,8},{10,11... | collective-permute-start | bytes 331784 | tf_op jit(solution)/shard_map/ppermute | solution.py:136
  78.4 7.4 %collective-permute-start.28 = (bf16[432,128]{1,0:T(8,128)(2,1)S(1)}, bf16[432,128]{1,0:T(8,128)(2,1)S(1)}, u32[]{:S(2)}, u32[]{:S(2)}) collective-permute-start(bf16[432,128]{1,0:T(8,128)(2,1)S(1)} %depth_sum.1.refs_0_), channel_id=1, source_target_pairs={{0,2},{1,3},{2,0},{3,1},{4,6},{5,7},{6,4},{7,5},{8,10},{9,11},{10,... | collective-permute-start | bytes 331784 | tf_op jit(solution)/shard_map/ppermute | solution.py:136
  (11 other events, 50.8 us)
where the time goes:
time: 86.6 us; the launch traced here: 86.5 us
  waiting for transfers between devices  37.3 us (43%)
  starting transfers between devices  32.5 us (38%)
  Pallas kernels  14.8 us (17%)
  local copies, waits for them, and re-layouts  0.96 us (1%)
  between operations  0.87 us (1%)
    ppermute x27, waiting for transfers between devices, swap(): return lax.ppermute(block, axes, [(i, i ^ distance) for i in range(count)])  36.3 us
    ppermute x27, starting transfers between devices, swap(): return lax.ppermute(block, axes, [(i, i ^ distance) for i in range(count)])  28.8 us
    pallas_call x23, Pallas kernels, call(): pl.pallas_call(kernel, name=name, out_shape=out_shapes, in_specs=[whole]...  14.8 us
    ppermute x1, starting transfers between devices, gathered_body(): z_a = lax.ppermute(send_a, 'gz', z_pairs[0])  3.09 us
  transfers between devices with their start and end apart: 29, of which 22 were waited for; matrix products, arithmetic and copies ran while one was open for 0% of the time, Pallas kernels for 8%

commit v1 on v0

--- a/solution.py
+++ b/solution.py
@@ -409,14 +409,13 @@
             window[quarter + g * span : quarter + (g + 1) * span, bc * wide : (bc + 1) * wide] = moved[
                 bc * span : (bc + 1) * span, :
             ]
-    both = pre = None
+    pre = matmul(window[2 * quarter :, :], w_bottle[18:].reshape(9 * wide, outs))
+    both = None
     for bc in range(9):
         part = slice(bc * wide, (bc + 1) * wide)
         weight = jnp.concatenate([w_bottle[bc], w_bottle[9 + bc]], axis=1)
         term = matmul(window[: cells + quarter, part], weight)
         both = term if both is None else both + term
-        term = matmul(window[2 * quarter :, part], w_bottle[18 + bc])
-        pre = term if pre is None else pre + term
     pre = pre + both[:cells, :outs] + both[quarter:, outs:]
     sig = jax.nn.sigmoid(pre)
     bottle[...] = (pre * sig).astype(BF16)

time: 86.6 us -> 86.7 us (level)
  no operation moved by 1% of the time
where the time goes in v1:
time: 86.7 us; the launch traced here: 86.6 us
  waiting for transfers between devices  37.3 us (43%)
  starting transfers between devices  32.6 us (38%)
  Pallas kernels  14.8 us (17%)
  local copies, waits for them, and re-layouts  0.96 us (1%)
  between operations  0.87 us (1%)
    ppermute x27, waiting for transfers between devices, swap(): return lax.ppermute(block, axes, [(i, i ^ distance) for i in range(count)])  36.2 us
    ppermute x27, starting transfers between devices, swap(): return lax.ppermute(block, axes, [(i, i ^ distance) for i in range(count)])  28.9 us
    pallas_call x23, Pallas kernels, call(): pl.pallas_call(kernel, name=name, out_shape=out_shapes, in_specs=[whole]...  14.8 us
    ppermute x1, starting transfers between devices, gathered_body(): z_a = lax.ppermute(send_a, 'gz', z_pairs[0])  3.09 us
  transfers between devices with their start and end apart: 29, of which 22 were waited for; matrix products, arithmetic and copies ran while one was open for 0% of the time, Pallas kernels for 8%

profile of v1, /device:TPU:0, one launch (start us, length us, event | category | flops | bytes accessed | tf_op | source)
XLA Modules:
  0.0 86.6 jit_solution(11799546815916228567)
XLA Ops:
  1.5 3.1 %collective-permute-start = (bf16[8,8,128]{2,1,0:T(8,128)(2,1)S(1)}, bf16[8,8,128]{2,1,0:T(8,128)(2,1)S(1)}, u32[]{:S(2)}, u32[]{:S(2)}) collective-permute-start(bf16[8,8,128]{2,1,0:T(8,128)(2,1)S(1)} %get-tuple-element.60), channel_id=1, source_target_pairs={{0,1},{1,0},{2,3},{3,2},{4,5},{5,4},{6,7},{7,6},{8,9},{9,8},{10,11... | collective-permute-start | bytes 49160 | tf_op jit(solution)/shard_map/ppermute | solution.py:645
  6.4 3.0 %collective-permute-start.3 = (bf16[16,128]{1,0:T(8,128)(2,1)S(1)}, bf16[16,128]{1,0:T(8,128)(2,1)S(1)}, u32[]{:S(2)}, u32[]{:S(2)}) collective-permute-start(bf16[16,128]{1,0:T(8,128)(2,1)S(1)} %get-tuple-element.63), channel_id=1, source_target_pairs={{0,24},{4,28},{8,16},{12,20},{16,8},{20,12},{24,0},{28,4},{1,25},{... | collective-permute-start | bytes 12296 | tf_op jit(solution)/shard_map/ppermute | solution.py:136
  11.0 2.8 %collective-permute-done.4.across = bf16[80,128]{1,0:T(8,128)(2,1)S(1)} collective-permute-done((bf16[80,128]{1,0:T(8,128)(2,1)S(1)}, bf16[80,128]{1,0:T(8,128)(2,1)S(1)}, u32[]{:S(2)}, u32[]{:S(2)}) %collective-permute-start.4) | collective-permute-done | bytes 20512 | tf_op jit(solution)/shard_map/ppermute | solution.py:136
  15.1 1.5 %hidden.1 = (bf16[8,64,128]{2,1,0:T(8,128)(2,1)S(1)}, f32[8,64,128]{2,1,0:T(8,128)S(1)}, bf16[10,128,128]{2,1,0:T(8,128)(2,1)S(1)}, bf16[64,640]{1,0:T(8,128)(2,...) custom-call(bf16[8,8,8,128]{3,2,1,0:T(8,128)(2,1)S(1)} %copy-done.10, ...), custom_call_target="tpu_custom_call" | custom-call | flops 2000000000 | bytes 2000000 | tf_op jit(solution)/shard_map/hidden/pallas_call | solution.py:18
  16.7 3.7 %collective-permute-start.6 = (bf16[64,640]{1,0:T(8,128)(2,1)S(1)}, bf16[64,640]{1,0:T(8,128)(2,1)S(1)}, u32[]{:S(2)}, u32[]{:S(2)}) collective-permute-start(bf16[64,640]{1,0:T(8,128)(2,1)S(1)} %get-tuple-element.71), channel_id=1, source_target_pairs={{0,3},{1,2},{2,1},{3,0},{4,7},{5,6},{6,5},{7,4},{8,11},{9,10},{10,... | collective-permute-start | bytes 245768 | tf_op jit(solution)/shard_map/ppermute | solution.py:136
  20.3 2.5 %collective-permute-start.7 = (bf16[64,640]{1,0:T(8,128)(2,1)S(1)}, bf16[64,640]{1,0:T(8,128)(2,1)S(1)}, u32[]{:S(2)}, u32[]{:S(2)}) collective-permute-start(bf16[64,640]{1,0:T(8,128)(2,1)S(1)} %get-tuple-element.72), channel_id=1, source_target_pairs={{0,2},{1,3},{2,0},{3,1},{4,6},{5,7},{6,4},{7,5},{8,10},{9,11},{10,... | collective-permute-start | bytes 245768 | tf_op jit(solution)/shard_map/ppermute | solution.py:136
  23.3 5.7 %collective-permute-done.7.refs_2_ = bf16[64,640]{1,0:T(8,128)(2,1)S(1)} collective-permute-done((bf16[64,640]{1,0:T(8,128)(2,1)S(1)}, bf16[64,640]{1,0:T(8,128)(2,1)S(1)}, u32[]{:S(2)}, u32[]{:S(2)}) %collective-permute-start.7) | collective-permute-done | bytes 81952 | tf_op jit(solution)/shard_map/ppermute | solution.py:136
  29.3 1.6 %collective-permute-start.10 = (bf16[16,512]{1,0:T(8,128)(2,1)S(1)}, bf16[16,512]{1,0:T(8,128)(2,1)S(1)}, u32[]{:S(2)}, u32[]{:S(2)}) collective-permute-start(bf16[16,512]{1,0:T(8,128)(2,1)S(1)} %get-tuple-element.82), channel_id=1, source_target_pairs={{0,24},{4,28},{8,16},{12,20},{16,8},{20,12},{24,0},{28,4},{1,25},{... | collective-permute-start | bytes 49160 | tf_op jit(solution)/shard_map/ppermute | solution.py:136
  31.4 1.5 %collective-permute-start.11 = (bf16[64,512]{1,0:T(8,128)(2,1)S(1)}, bf16[64,512]{1,0:T(8,128)(2,1)S(1)}, u32[]{:S(2)}, u32[]{:S(2)}) collective-permute-start(bf16[64,512]{1,0:T(8,128)(2,1)S(1)} %get-tuple-element.83), channel_id=1, source_target_pairs={{0,8},{4,12},{8,0},{12,4},{16,24},{20,28},{24,16},{28,20},{1,9},{5... | collective-permute-start | bytes 196616 | tf_op jit(solution)/shard_map/ppermute | solution.py:136
  32.9 1.3 %collective-permute-done.10.block = bf16[16,512]{1,0:T(8,128)(2,1)S(1)} collective-permute-done((bf16[16,512]{1,0:T(8,128)(2,1)S(1)}, bf16[16,512]{1,0:T(8,128)(2,1)S(1)}, u32[]{:S(2)}, u32[]{:S(2)}) %collective-permute-start.10) | collective-permute-done | bytes 16416 | tf_op jit(solution)/shard_map/ppermute | solution.py:136
  35.9 1.2 %collective-permute-done.12.refs_3_ = bf16[160,512]{1,0:T(8,128)(2,1)S(1)} collective-permute-done((bf16[160,512]{1,0:T(8,128)(2,1)S(1)}, bf16[160,512]{1,0:T(8,128)(2,1)S(1)}, u32[]{:S(2)}, u32[]{:S(2)}) %collective-permute-start.12) | collective-permute-done | bytes 163872 | tf_op jit(solution)/shard_map/ppermute | solution.py:136
  37.1 2.1 %bottle.1 = (bf16[256,128]{1,0:T(8,128)(2,1)S(1)}, bf16[512,128]{1,0:T(8,128)(2,1)S(1)}, bf16[512,128]{1,0:T(8,128)(2,1)S(1)}, bf16[512,128]{1,0:T(8,128)(2,1)S(1)}, bf16[512,128]{1,0:T(8,128)(2,1)S(1)}) custom-call(bf16[256,512]{1,0:T(8,128)(2,1)S(1)} %get-tuple-element.79.refs_0_, bf16[256,128]{1,0:T(8,128)(2,1)S(1)} %get-tuple-element.80.refs_1_, ...), custom_call_target="tpu_custom_call" | custom-call | flops 2000000000 | bytes 2000000 | tf_op jit(solution)/shard_map/bottle/pallas_call | solution.py:18
  39.3 2.5 %collective-permute-start.13 = (bf16[512,128]{1,0:T(8,128)(2,1)S(1)}, bf16[512,128]{1,0:T(8,128)(2,1)S(1)}, u32[]{:S(2)}, u32[]{:S(2)}) collective-permute-start(bf16[512,128]{1,0:T(8,128)(2,1)S(1)} %get-tuple-element.90), channel_id=1, source_target_pairs={{0,24},{4,28},{8,16},{12,20},{16,8},{20,12},{24,0},{28,4},{1,25},{... | collective-permute-start | bytes 393224 | tf_op jit(solution)/shard_map/ppermute | solution.py:136
  42.8 3.2 %collective-permute-done.13.refs_2_.refs_7_.refs_6_ = bf16[512,128]{1,0:T(8,128)(2,1)S(1)} collective-permute-done((bf16[512,128]{1,0:T(8,128)(2,1)S(1)}, bf16[512,128]{1,0:T(8,128)(2,1)S(1)}, u32[]{:S(2)}, u32[]{:S(2)}) %collective-permute-start.13) | collective-permute-done | bytes 131104 | tf_op jit(solution)/shard_map/ppermute | solution.py:136
  46.1 2.5 %collective-permute-done.15.refs_4_.refs_5_ = bf16[512,128]{1,0:T(8,128)(2,1)S(1)} collective-permute-done((bf16[512,128]{1,0:T(8,128)(2,1)S(1)}, bf16[512,128]{1,0:T(8,128)(2,1)S(1)}, u32[]{:S(2)}, u32[]{:S(2)}) %collective-permute-start.15) | collective-permute-done | bytes 131104 | tf_op jit(solution)/shard_map/ppermute | solution.py:136
  50.1 1.6 %coarse_grad.1 = (bf16[64,640]{1,0:T(8,128)(2,1)S(1)}, bf16[64,640]{1,0:T(8,128)(2,1)S(1)}, bf16[64,640]{1,0:T(8,128)(2,1)S(1)}, bf16[64,640]{1,0:T(8,128)(2,1)S(1)}) custom-call(bf16[512,128]{1,0:T(8,128)(2,1)S(1)} %get-tuple-element.102.refs_0_.refs_1_, bf16[512,128]{1,0:T(8,128)(2,1)S(1)} %collective-permute-done.14.refs_1_.refs_8_.refs_7_, ...), custom_call_target="tpu_custom_call" | custom-call | flops 300000000 | bytes 300000 | tf_op jit(solution)/shard_map/coarse_grad/pallas_call | solution.py:18
  51.8 2.9 %collective-permute-start.20 = (bf16[64,640]{1,0:T(8,128)(2,1)S(1)}, bf16[64,640]{1,0:T(8,128)(2,1)S(1)}, u32[]{:S(2)}, u32[]{:S(2)}) collective-permute-start(bf16[64,640]{1,0:T(8,128)(2,1)S(1)} %get-tuple-element.95), channel_id=1, source_target_pairs={{0,3},{1,2},{2,1},{3,0},{4,7},{5,6},{6,5},{7,4},{8,11},{9,10},{10,... | collective-permute-start | bytes 245768 | tf_op jit(solution)/shard_map/ppermute | solution.py:136
  54.7 1.5 %collective-permute-start.22 = (bf16[64,640]{1,0:T(8,128)(2,1)S(1)}, bf16[64,640]{1,0:T(8,128)(2,1)S(1)}, u32[]{:S(2)}, u32[]{:S(2)}) collective-permute-start(bf16[64,640]{1,0:T(8,128)(2,1)S(1)} %get-tuple-element.97), channel_id=1, source_target_pairs={{0,1},{1,0},{2,3},{3,2},{4,5},{5,4},{6,7},{7,6},{8,9},{9,8},{10,11... | collective-permute-start | bytes 245768 | tf_op jit(solution)/shard_map/ppermute | solution.py:136
  57.9 1.1 %collective-permute-done.20.refs_1_ = bf16[64,640]{1,0:T(8,128)(2,1)S(1)} collective-permute-done((bf16[64,640]{1,0:T(8,128)(2,1)S(1)}, bf16[64,640]{1,0:T(8,128)(2,1)S(1)}, u32[]{:S(2)}, u32[]{:S(2)}) %collective-permute-start.20) | collective-permute-done | bytes 81952 | tf_op jit(solution)/shard_map/ppermute | solution.py:136
  59.0 2.8 %collective-permute-done.21.refs_2_ = bf16[64,640]{1,0:T(8,128)(2,1)S(1)} collective-permute-done((bf16[64,640]{1,0:T(8,128)(2,1)S(1)}, bf16[64,640]{1,0:T(8,128)(2,1)S(1)}, u32[]{:S(2)}, u32[]{:S(2)}) %collective-permute-start.21) | collective-permute-done | bytes 81952 | tf_op jit(solution)/shard_map/ppermute | solution.py:136
  61.8 1.1 %hidden_grad.1 = (bf16[640,384]{1,0:T(8,128)(2,1)S(1)}, bf16[64,512]{1,0:T(8,128)(2,1)S(1)}, bf16[4,432,128]{2,1,0:T(8,128)(2,1)S(1)}) custom-call(bf16[64,640]{1,0:T(8,128)(2,1)S(1)} %get-tuple-element.94.refs_0_, bf16[64,640]{1,0:T(8,128)(2,1)S(1)} %collective-permute-done.20.refs_1_, bf16[64,640]{1,0:T(8,128)(2,1)S(1)} %collective-permute-done.21.refs_2_, ...), custom_call_target="tpu_custom_call" | custom-call | flops 300000000 | bytes 300000 | tf_op jit(solution)/shard_map/hidden_grad/pallas_call | solution.py:18
  63.6 1.2 %collective-permute-done.23.got = bf16[4,432,128]{2,1,0:T(8,128)(2,1)S(1)} collective-permute-done((bf16[4,432,128]{2,1,0:T(8,128)(2,1)S(1)}, bf16[4,432,128]{2,1,0:T(8,128)(2,1)S(1)}, u32[]{:S(2)}, u32[]{:S(2)}) %collective-permute-start.23) | collective-permute-done | bytes 442400 | tf_op jit(solution)/shard_map/ppermute | solution.py:136
  64.9 1.8 %collective-permute-start.24 = (bf16[432,128]{1,0:T(8,128)(2,1)S(1)}, bf16[432,128]{1,0:T(8,128)(2,1)S(1)}, u32[]{:S(2)}, u32[]{:S(2)}) collective-permute-start(bf16[432,128]{1,0:T(8,128)(2,1)S(1)} %get-tuple-element.107), channel_id=1, source_target_pairs={{0,24},{4,28},{8,16},{12,20},{16,8},{20,12},{24,0},{28,4},{1,25},{... | collective-permute-start | bytes 331784 | tf_op jit(solution)/shard_map/ppermute | solution.py:136
  66.7 1.2 %collective-permute-start.25 = (bf16[432,128]{1,0:T(8,128)(2,1)S(1)}, bf16[432,128]{1,0:T(8,128)(2,1)S(1)}, u32[]{:S(2)}, u32[]{:S(2)}) collective-permute-start(bf16[432,128]{1,0:T(8,128)(2,1)S(1)} %get-tuple-element.108), channel_id=1, source_target_pairs={{0,16},{4,20},{8,24},{12,28},{16,0},{20,4},{24,8},{28,12},{1,17},{... | collective-permute-start | bytes 331784 | tf_op jit(solution)/shard_map/ppermute | solution.py:136
  68.4 1.1 %output.1 = bf16[8,8,8,128]{3,2,1,0:T(8,128)(2,1)} custom-call(bf16[64,512]{1,0:T(8,128)(2,1)S(1)} %get-tuple-element.110.bottle, bf16[8,64,128]{2,1,0:T(8,128)(2,1)S(1)} %get-tuple-element.111.hidden, bf16[8,512,128]{2,1,0:T(8,128)(2,1)S(1)} %copy-done, bf16[64,64]{1,0:T(8,128)(2,1)S(1)} %copy-done.6), custom_call_target="tpu_custom_call" | custom-call | flops 300000000 | bytes 300000 | tf_op jit(solution)/shard_map/output/pallas_call | solution.py:18
  69.6 2.0 %collective-permute-done.24.refs_1_ = bf16[432,128]{1,0:T(8,128)(2,1)S(1)} collective-permute-done((bf16[432,128]{1,0:T(8,128)(2,1)S(1)}, bf16[432,128]{1,0:T(8,128)(2,1)S(1)}, u32[]{:S(2)}, u32[]{:S(2)}) %collective-permute-start.24) | collective-permute-done | bytes 110624 | tf_op jit(solution)/shard_map/ppermute | solution.py:136
  71.6 1.7 %collective-permute-done.25.refs_2_ = bf16[432,128]{1,0:T(8,128)(2,1)S(1)} collective-permute-done((bf16[432,128]{1,0:T(8,128)(2,1)S(1)}, bf16[432,128]{1,0:T(8,128)(2,1)S(1)}, u32[]{:S(2)}, u32[]{:S(2)}) %collective-permute-start.25) | collective-permute-done | bytes 110624 | tf_op jit(solution)/shard_map/ppermute | solution.py:136
  73.4 1.2 %collective-permute-start.27 = (bf16[432,128]{1,0:T(8,128)(2,1)S(1)}, bf16[432,128]{1,0:T(8,128)(2,1)S(1)}, u32[]{:S(2)}, u32[]{:S(2)}) collective-permute-start(bf16[432,128]{1,0:T(8,128)(2,1)S(1)} %plane_sum.1.refs_0_), channel_id=1, source_target_pairs={{0,1},{1,0},{2,3},{3,2},{4,5},{5,4},{6,7},{7,6},{8,9},{9,8},{10,11... | collective-permute-start | bytes 331784 | tf_op jit(solution)/shard_map/ppermute | solution.py:136
  74.8 3.6 %collective-permute-done.27.refs_1_ = bf16[432,128]{1,0:T(8,128)(2,1)S(1)} collective-permute-done((bf16[432,128]{1,0:T(8,128)(2,1)S(1)}, bf16[432,128]{1,0:T(8,128)(2,1)S(1)}, u32[]{:S(2)}, u32[]{:S(2)}) %collective-permute-start.27) | collective-permute-done | bytes 110624 | tf_op jit(solution)/shard_map/ppermute | solution.py:136
  78.5 1.5 %collective-permute-start.28 = (bf16[432,128]{1,0:T(8,128)(2,1)S(1)}, bf16[432,128]{1,0:T(8,128)(2,1)S(1)}, u32[]{:S(2)}, u32[]{:S(2)}) collective-permute-start(bf16[432,128]{1,0:T(8,128)(2,1)S(1)} %depth_sum.1.refs_0_), channel_id=1, source_target_pairs={{0,2},{1,3},{2,0},{3,1},{4,6},{5,7},{6,4},{7,5},{8,10},{9,11},{10,... | collective-permute-start | bytes 331784 | tf_op jit(solution)/shard_map/ppermute | solution.py:136
  80.0 2.9 %grad_bottle.1 = f32[27,64,128]{2,1,0:T(8,128)} custom-call(bf16[1152,1024]{1,0:T(8,128)(2,1)S(1)} %coarse_transpose.1.turned, bf16[1024,640]{1,0:T(8,128)(2,1)S(1)} %wide.1), custom_call_target="tpu_custom_call" | custom-call | flops 4000000000 | bytes 4000000 | tf_op jit(solution)/shard_map/grad_bottle/pallas_call | solution.py:18
  82.9 3.0 %collective-permute-done.28.refs_1_ = bf16[432,128]{1,0:T(8,128)(2,1)S(1)} collective-permute-done((bf16[432,128]{1,0:T(8,128)(2,1)S(1)}, bf16[432,128]{1,0:T(8,128)(2,1)S(1)}, u32[]{:S(2)}, u32[]{:S(2)}) %collective-permute-start.28) | collective-permute-done | bytes 110624 | tf_op jit(solution)/shard_map/ppermute | solution.py:136
  (77 shorter events, 15.2 us)
Async XLA Ops:
  1.5 4.8 %collective-permute-start = (bf16[8,8,128]{2,1,0:T(8,128)(2,1)S(1)}, bf16[8,8,128]{2,1,0:T(8,128)(2,1)S(1)}, u32[]{:S(2)}, u32[]{:S(2)}) collective-permute-start(bf16[8,8,128]{2,1,0:T(8,128)(2,1)S(1)} %get-tuple-element.60), channel_id=1, source_target_pairs={{0,1},{1,0},{2,3},{3,2},{4,5},{5,4},{6,7},{7,6},{8,9},{9,8},{10,11... | collective-permute-start | bytes 49160 | tf_op jit(solution)/shard_map/ppermute | solution.py:645
  4.6 1.7 %collective-permute-start.1 = (bf16[8,8,128]{2,1,0:T(8,128)(2,1)S(1)}, bf16[8,8,128]{2,1,0:T(8,128)(2,1)S(1)}, u32[]{:S(2)}, u32[]{:S(2)}) collective-permute-start(bf16[8,8,128]{2,1,0:T(8,128)(2,1)S(1)} %get-tuple-element.61), channel_id=1, source_target_pairs={{1,2},{2,1},{5,6},{6,5},{9,10},{10,9},{13,14},{14,13},{17,18},{18,... | collective-permute-start | bytes 49160 | tf_op jit(solution)/shard_map/ppermute | solution.py:644
  6.4 4.6 %collective-permute-start.3 = (bf16[16,128]{1,0:T(8,128)(2,1)S(1)}, bf16[16,128]{1,0:T(8,128)(2,1)S(1)}, u32[]{:S(2)}, u32[]{:S(2)}) collective-permute-start(bf16[16,128]{1,0:T(8,128)(2,1)S(1)} %get-tuple-element.63), channel_id=1, source_target_pairs={{0,24},{4,28},{8,16},{12,20},{16,8},{20,12},{24,0},{28,4},{1,25},{... | collective-permute-start | bytes 12296 | tf_op jit(solution)/shard_map/ppermute | solution.py:136
  9.4 4.4 %collective-permute-start.2 = (bf16[128,128]{1,0:T(8,128)(2,1)S(1)}, bf16[128,128]{1,0:T(8,128)(2,1)S(1)}, u32[]{:S(2)}, u32[]{:S(2)}) collective-permute-start(bf16[128,128]{1,0:T(8,128)(2,1)S(1)} %get-tuple-element.62), channel_id=1, source_target_pairs={{0,16},{4,20},{8,24},{12,28},{16,0},{20,4},{24,8},{28,12},{1,17},{... | collective-permute-start | bytes 98312 | tf_op jit(solution)/shard_map/ppermute | solution.py:136
  9.9 3.8 %collective-permute-start.4 = (bf16[80,128]{1,0:T(8,128)(2,1)S(1)}, bf16[80,128]{1,0:T(8,128)(2,1)S(1)}, u32[]{:S(2)}, u32[]{:S(2)}) collective-permute-start(bf16[80,128]{1,0:T(8,128)(2,1)S(1)} %get-tuple-element.64), channel_id=1, source_target_pairs={{0,8},{4,12},{8,0},{12,4},{16,24},{20,28},{24,16},{28,20},{1,9},{5... | collective-permute-start | bytes 61448 | tf_op jit(solution)/shard_map/ppermute | solution.py:136
  13.8 1.3 %collective-permute-start.5 = (bf16[192,128]{1,0:T(8,128)(2,1)S(1)}, bf16[192,128]{1,0:T(8,128)(2,1)S(1)}, u32[]{:S(2)}, u32[]{:S(2)}) collective-permute-start(bf16[192,128]{1,0:T(8,128)(2,1)S(1)} %relay_rims.2), channel_id=1, source_target_pairs={{0,4},{4,0},{8,12},{12,8},{16,20},{20,16},{24,28},{28,24},{1,5},{5... | collective-permute-start | bytes 147464 | tf_op jit(solution)/shard_map/ppermute | solution.py:136
  15.1 13.9 %copy-start.12 = (bf16[2,224,256]{2,1,0:T(8,128)(2,1)S(1)}, bf16[2,224,256]{2,1,0:T(8,128)(2,1)}, u32[]{:S(2)}) copy-start(bf16[2,224,256]{2,1,0:T(8,128)(2,1)} %constant.19.clone.refs_4_) | copy-start | bytes 688132
  16.7 6.7 %collective-permute-start.6 = (bf16[64,640]{1,0:T(8,128)(2,1)S(1)}, bf16[64,640]{1,0:T(8,128)(2,1)S(1)}, u32[]{:S(2)}, u32[]{:S(2)}) collective-permute-start(bf16[64,640]{1,0:T(8,128)(2,1)S(1)} %get-tuple-element.71), channel_id=1, source_target_pairs={{0,3},{1,2},{2,1},{3,0},{4,7},{5,6},{6,5},{7,4},{8,11},{9,10},{10,... | collective-permute-start | bytes 245768 | tf_op jit(solution)/shard_map/ppermute | solution.py:136
  20.3 8.7 %collective-permute-start.7 = (bf16[64,640]{1,0:T(8,128)(2,1)S(1)}, bf16[64,640]{1,0:T(8,128)(2,1)S(1)}, u32[]{:S(2)}, u32[]{:S(2)}) collective-permute-start(bf16[64,640]{1,0:T(8,128)(2,1)S(1)} %get-tuple-element.72), channel_id=1, source_target_pairs={{0,2},{1,3},{2,0},{3,1},{4,6},{5,7},{6,4},{7,5},{8,10},{9,11},{10,... | collective-permute-start | bytes 245768 | tf_op jit(solution)/shard_map/ppermute | solution.py:136
  22.9 6.2 %collective-permute-start.8 = (bf16[64,640]{1,0:T(8,128)(2,1)S(1)}, bf16[64,640]{1,0:T(8,128)(2,1)S(1)}, u32[]{:S(2)}, u32[]{:S(2)}) collective-permute-start(bf16[64,640]{1,0:T(8,128)(2,1)S(1)} %get-tuple-element.73), channel_id=1, source_target_pairs={{0,1},{1,0},{2,3},{3,2},{4,5},{5,4},{6,7},{7,6},{8,9},{9,8},{10,11... | collective-permute-start | bytes 245768 | tf_op jit(solution)/shard_map/ppermute | solution.py:136
  29.3 4.9 %collective-permute-start.10 = (bf16[16,512]{1,0:T(8,128)(2,1)S(1)}, bf16[16,512]{1,0:T(8,128)(2,1)S(1)}, u32[]{:S(2)}, u32[]{:S(2)}) collective-permute-start(bf16[16,512]{1,0:T(8,128)(2,1)S(1)} %get-tuple-element.82), channel_id=1, source_target_pairs={{0,24},{4,28},{8,16},{12,20},{16,8},{20,12},{24,0},{28,4},{1,25},{... | collective-permute-start | bytes 49160 | tf_op jit(solution)/shard_map/ppermute | solution.py:136
  30.9 4.3 %collective-permute-start.9 = (bf16[64,512]{1,0:T(8,128)(2,1)S(1)}, bf16[64,512]{1,0:T(8,128)(2,1)S(1)}, u32[]{:S(2)}, u32[]{:S(2)}) collective-permute-start(bf16[64,512]{1,0:T(8,128)(2,1)S(1)} %get-tuple-element.81), channel_id=1, source_target_pairs={{0,16},{4,20},{8,24},{12,28},{16,0},{20,4},{24,8},{28,12},{1,17},{... | collective-permute-start | bytes 196616 | tf_op jit(solution)/shard_map/ppermute | solution.py:136
  31.4 4.3 %collective-permute-start.11 = (bf16[64,512]{1,0:T(8,128)(2,1)S(1)}, bf16[64,512]{1,0:T(8,128)(2,1)S(1)}, u32[]{:S(2)}, u32[]{:S(2)}) collective-permute-start(bf16[64,512]{1,0:T(8,128)(2,1)S(1)} %get-tuple-element.83), channel_id=1, source_target_pairs={{0,8},{4,12},{8,0},{12,4},{16,24},{20,28},{24,16},{28,20},{1,9},{5... | collective-permute-start | bytes 196616 | tf_op jit(solution)/shard_map/ppermute | solution.py:136
  35.7 1.5 %collective-permute-start.12 = (bf16[160,512]{1,0:T(8,128)(2,1)S(1)}, bf16[160,512]{1,0:T(8,128)(2,1)S(1)}, u32[]{:S(2)}, u32[]{:S(2)}) collective-permute-start(bf16[160,512]{1,0:T(8,128)(2,1)S(1)} %relay_rims.3), channel_id=1, source_target_pairs={{0,4},{4,0},{8,12},{12,8},{16,20},{20,16},{24,28},{28,24},{1,5},{5... | collective-permute-start | bytes 491528 | tf_op jit(solution)/shard_map/ppermute | solution.py:136
  37.1 13.0 %copy-start.2 = (bf16[1152,128]{1,0:T(8,128)(2,1)S(1)}, bf16[1152,128]{1,0:T(8,128)(2,1)}, u32[]{:S(2)}) copy-start(bf16[1152,128]{1,0:T(8,128)(2,1)} %constant.18.clone.refs_9_.refs_0_) | copy-start | bytes 884740
  39.3 6.8 %collective-permute-start.13 = (bf16[512,128]{1,0:T(8,128)(2,1)S(1)}, bf16[512,128]{1,0:T(8,128)(2,1)S(1)}, u32[]{:S(2)}, u32[]{:S(2)}) collective-permute-start(bf16[512,128]{1,0:T(8,128)(2,1)S(1)} %get-tuple-element.90), channel_id=1, source_target_pairs={{0,24},{4,28},{8,16},{12,20},{16,8},{20,12},{24,0},{28,4},{1,25},{... | collective-permute-start | bytes 393224 | tf_op jit(solution)/shard_map/ppermute | solution.py:136
  41.8 6.8 %collective-permute-start.15 = (bf16[512,128]{1,0:T(8,128)(2,1)S(1)}, bf16[512,128]{1,0:T(8,128)(2,1)S(1)}, u32[]{:S(2)}, u32[]{:S(2)}) collective-permute-start(bf16[512,128]{1,0:T(8,128)(2,1)S(1)} %get-tuple-element.91), channel_id=1, source_target_pairs={{0,16},{4,20},{8,24},{12,28},{16,0},{20,4},{24,8},{28,12},{1,17},{... | collective-permute-start | bytes 393224 | tf_op jit(solution)/shard_map/ppermute | solution.py:136
  42.3 6.4 %collective-permute-start.17 = (bf16[512,128]{1,0:T(8,128)(2,1)S(1)}, bf16[512,128]{1,0:T(8,128)(2,1)S(1)}, u32[]{:S(2)}, u32[]{:S(2)}) collective-permute-start(bf16[512,128]{1,0:T(8,128)(2,1)S(1)} %get-tuple-element.92), channel_id=1, source_target_pairs={{0,8},{4,12},{8,0},{12,4},{16,24},{20,28},{24,16},{28,20},{1,9},{5... | collective-permute-start | bytes 393224 | tf_op jit(solution)/shard_map/ppermute | solution.py:136
  42.8 6.3 %collective-permute-start.19 = (bf16[512,128]{1,0:T(8,128)(2,1)S(1)}, bf16[512,128]{1,0:T(8,128)(2,1)S(1)}, u32[]{:S(2)}, u32[]{:S(2)}) collective-permute-start(bf16[512,128]{1,0:T(8,128)(2,1)S(1)} %get-tuple-element.102.refs_0_.refs_1_), channel_id=1, source_target_pairs={{0,4},{4,0},{8,12},{12,8},{16,20},{20,16},{24,28},{28,24},{1,5},{5... | collective-permute-start | bytes 393224 | tf_op jit(solution)/shard_map/ppermute | solution.py:136
  46.1 3.0 %collective-permute-start.14 = (bf16[512,128]{1,0:T(8,128)(2,1)S(1)}, bf16[512,128]{1,0:T(8,128)(2,1)S(1)}, u32[]{:S(2)}, u32[]{:S(2)}) collective-permute-start(bf16[512,128]{1,0:T(8,128)(2,1)S(1)} %collective-permute-done.13.refs_2_.refs_7_.refs_6_), channel_id=1, source_target_pairs={{0,4},{4,0},{8,12},{12,8},{16,20},{20,16},{24,28},{28,24},{1,5},{5... | collective-permute-start | bytes 393224 | tf_op jit(solution)/shard_map/ppermute | solution.py:136
  48.6 1.3 %collective-permute-start.16 = (bf16[512,128]{1,0:T(8,128)(2,1)S(1)}, bf16[512,128]{1,0:T(8,128)(2,1)S(1)}, u32[]{:S(2)}, u32[]{:S(2)}) collective-permute-start(bf16[512,128]{1,0:T(8,128)(2,1)S(1)} %collective-permute-done.15.refs_4_.refs_5_), channel_id=1, source_target_pairs={{0,4},{4,0},{8,12},{12,8},{16,20},{20,16},{24,28},{28,24},{1,5},{5... | collective-permute-start | bytes 393224 | tf_op jit(solution)/shard_map/ppermute | solution.py:136
  48.7 1.5 %collective-permute-start.18 = (bf16[512,128]{1,0:T(8,128)(2,1)S(1)}, bf16[512,128]{1,0:T(8,128)(2,1)S(1)}, u32[]{:S(2)}, u32[]{:S(2)}) collective-permute-start(bf16[512,128]{1,0:T(8,128)(2,1)S(1)} %collective-permute-done.17.refs_6_.refs_3_.refs_2_), channel_id=1, source_target_pairs={{0,4},{4,0},{8,12},{12,8},{16,20},{20,16},{24,28},{28,24},{1,5},{5... | collective-permute-start | bytes 393224 | tf_op jit(solution)/shard_map/ppermute | solution.py:136
  50.1 6.1 %copy-start.4 = (bf16[256,1152]{1,0:T(8,128)(2,1)S(1)}, bf16[256,1152]{1,0:T(8,128)(2,1)}, u32[]{:S(2)}) copy-start(bf16[256,1152]{1,0:T(8,128)(2,1)} %constant.17.clone.refs_1_) | copy-start | bytes 1769476
  51.8 7.2 %collective-permute-start.20 = (bf16[64,640]{1,0:T(8,128)(2,1)S(1)}, bf16[64,640]{1,0:T(8,128)(2,1)S(1)}, u32[]{:S(2)}, u32[]{:S(2)}) collective-permute-start(bf16[64,640]{1,0:T(8,128)(2,1)S(1)} %get-tuple-element.95), channel_id=1, source_target_pairs={{0,3},{1,2},{2,1},{3,0},{4,7},{5,6},{6,5},{7,4},{8,11},{9,10},{10,... | collective-permute-start | bytes 245768 | tf_op jit(solution)/shard_map/ppermute | solution.py:136
  54.7 7.1 %collective-permute-start.21 = (bf16[64,640]{1,0:T(8,128)(2,1)S(1)}, bf16[64,640]{1,0:T(8,128)(2,1)S(1)}, u32[]{:S(2)}, u32[]{:S(2)}) collective-permute-start(bf16[64,640]{1,0:T(8,128)(2,1)S(1)} %get-tuple-element.96), channel_id=1, source_target_pairs={{0,2},{1,3},{2,0},{3,1},{4,6},{5,7},{6,4},{7,5},{8,10},{9,11},{10,... | collective-permute-start | bytes 245768 | tf_op jit(solution)/shard_map/ppermute | solution.py:136
  54.7 7.1 %collective-permute-start.22 = (bf16[64,640]{1,0:T(8,128)(2,1)S(1)}, bf16[64,640]{1,0:T(8,128)(2,1)S(1)}, u32[]{:S(2)}, u32[]{:S(2)}) collective-permute-start(bf16[64,640]{1,0:T(8,128)(2,1)S(1)} %get-tuple-element.97), channel_id=1, source_target_pairs={{0,1},{1,0},{2,3},{3,2},{4,5},{5,4},{6,7},{7,6},{8,9},{9,8},{10,11... | collective-permute-start | bytes 245768 | tf_op jit(solution)/shard_map/ppermute | solution.py:136
  62.9 1.9 %collective-permute-start.23 = (bf16[4,432,128]{2,1,0:T(8,128)(2,1)S(1)}, bf16[4,432,128]{2,1,0:T(8,128)(2,1)S(1)}, u32[]{:S(2)}, u32[]{:S(2)}) collective-permute-start(bf16[4,432,128]{2,1,0:T(8,128)(2,1)S(1)} %get-tuple-element.105), channel_id=1, source_target_pairs={{0,4},{4,0},{8,12},{12,8},{16,20},{20,16},{24,28},{28,24},{1,5},{5... | collective-permute-start | bytes 1327112 | tf_op jit(solution)/shard_map/ppermute | solution.py:136
  64.9 6.7 %collective-permute-start.24 = (bf16[432,128]{1,0:T(8,128)(2,1)S(1)}, bf16[432,128]{1,0:T(8,128)(2,1)S(1)}, u32[]{:S(2)}, u32[]{:S(2)}) collective-permute-start(bf16[432,128]{1,0:T(8,128)(2,1)S(1)} %get-tuple-element.107), channel_id=1, source_target_pairs={{0,24},{4,28},{8,16},{12,20},{16,8},{20,12},{24,0},{28,4},{1,25},{... | collective-permute-start | bytes 331784 | tf_op jit(solution)/shard_map/ppermute | solution.py:136
  66.7 6.6 %collective-permute-start.25 = (bf16[432,128]{1,0:T(8,128)(2,1)S(1)}, bf16[432,128]{1,0:T(8,128)(2,1)S(1)}, u32[]{:S(2)}, u32[]{:S(2)}) collective-permute-start(bf16[432,128]{1,0:T(8,128)(2,1)S(1)} %get-tuple-element.108), channel_id=1, source_target_pairs={{0,16},{4,20},{8,24},{12,28},{16,0},{20,4},{24,8},{28,12},{1,17},{... | collective-permute-start | bytes 331784 | tf_op jit(solution)/shard_map/ppermute | solution.py:136
  67.9 5.5 %collective-permute-start.26 = (bf16[432,128]{1,0:T(8,128)(2,1)S(1)}, bf16[432,128]{1,0:T(8,128)(2,1)S(1)}, u32[]{:S(2)}, u32[]{:S(2)}) collective-permute-start(bf16[432,128]{1,0:T(8,128)(2,1)S(1)} %get-tuple-element.109), channel_id=1, source_target_pairs={{0,8},{4,12},{8,0},{12,4},{16,24},{20,28},{24,16},{28,20},{1,9},{5... | collective-permute-start | bytes 331784 | tf_op jit(solution)/shard_map/ppermute | solution.py:136
  73.4 5.0 %collective-permute-start.27 = (bf16[432,128]{1,0:T(8,128)(2,1)S(1)}, bf16[432,128]{1,0:T(8,128)(2,1)S(1)}, u32[]{:S(2)}, u32[]{:S(2)}) collective-permute-start(bf16[432,128]{1,0:T(8,128)(2,1)S(1)} %plane_sum.1.refs_0_), channel_id=1, source_target_pairs={{0,1},{1,0},{2,3},{3,2},{4,5},{5,4},{6,7},{7,6},{8,9},{9,8},{10,11... | collective-permute-start | bytes 331784 | tf_op jit(solution)/shard_map/ppermute | solution.py:136
  78.5 7.4 %collective-permute-start.28 = (bf16[432,128]{1,0:T(8,128)(2,1)S(1)}, bf16[432,128]{1,0:T(8,128)(2,1)S(1)}, u32[]{:S(2)}, u32[]{:S(2)}) collective-permute-start(bf16[432,128]{1,0:T(8,128)(2,1)S(1)} %depth_sum.1.refs_0_), channel_id=1, source_target_pairs={{0,2},{1,3},{2,0},{3,1},{4,6},{5,7},{6,4},{7,5},{8,10},{9,11},{10,... | collective-permute-start | bytes 331784 | tf_op jit(solution)/shard_map/ppermute | solution.py:136
  (11 other events, 50.8 us)
